TPU v7x, 32 devices: a whole 2x2x4 slice. The times are simulated.
32 devices in a mesh: ctx: 16 (over z, x, core), fsdp: 2 (over y).
Axes of the slice: x: 2, y: 2, z: 4, core: 2. Of those that a mesh axis runs over, the one named last changes fastest.
Arguments:
- tokens: bfloat16 [12, 2048, 576], P('fsdp', 'ctx'), may hold values from -6 to 6
- cotangent: bfloat16 [12, 2048, 576], P('fsdp', 'ctx'), may hold values from -8 to 8
- pair_order: int32 [12, 16], P('fsdp'), may hold values from 0 to 15, each once within a row
- query_weight: float32 [576, 576], P('fsdp', 'ctx'), may hold values from -0.5 to 0.5
- key_master_weight: float32 [576, 192], P('fsdp', 'ctx'), may hold values from -0.25 to 0.25
- value_master_weight: float32 [576, 192], P('fsdp', 'ctx'), may hold values from -0.25 to 0.25
- output_weight: float32 [576, 576], P('fsdp', 'ctx'), may hold values from -1.5 to 1.5
- gate_weight: float32 [576, 1536], P('fsdp', 'ctx'), may hold values from -0.25 to 0.25
- up_weight: float32 [576, 1536], P('fsdp', 'ctx'), may hold values from -0.25 to 0.25
- down_weight: float32 [1536, 576], P('fsdp', 'ctx'), may hold values from -0.21875 to 0.21875
- norm_gains: float32 [576, 2], P('fsdp'), may hold values from 0.5 to 1.5
- query_first: float32 [576, 576], P('fsdp', 'ctx'), may hold values from -224 to 224
- key_first_moment: float32 [576, 192], P('fsdp', 'ctx'), may hold values from -448 to 448
- value_first_moment: float32 [576, 192], P('fsdp', 'ctx'), may hold values from -320 to 320
- output_first: float32 [576, 576], P('fsdp', 'ctx'), may hold values from -20 to 20
- gate_first: float32 [576, 1536], P('fsdp', 'ctx'), may hold values from -56 to 56
- up_first: float32 [576, 1536], P('fsdp', 'ctx'), may hold values from -56 to 56
- down_first: float32 [1536, 576], P('fsdp', 'ctx'), may hold values from -64 to 64
- gains_first: float32 [576, 2], P('fsdp'), may hold values from -256 to 256
- query_second: float32 [576, 576], P('fsdp', 'ctx'), may hold values from 5160.96 to 20643.84
- key_second_moment: float32 [576, 192], P('fsdp', 'ctx'), may hold values from 20643.84 to 82821.12
- value_second_moment: float32 [576, 192], P('fsdp', 'ctx'), may hold values from 11550.72 to 46448.64
- output_second: float32 [576, 576], P('fsdp', 'ctx'), may hold values from 51.6096 to 206.4384
- gate_second: float32 [576, 1536], P('fsdp', 'ctx'), may hold values from 321.9456 to 1292.6976
- up_second: float32 [576, 1536], P('fsdp', 'ctx'), may hold values from 321.9456 to 1292.6976
- down_second: float32 [1536, 576], P('fsdp', 'ctx'), may hold values from 464.4864 to 1862.8608
- gains_second: float32 [576, 2], P('fsdp'), may hold values from 454.656 to 1818.624
Outputs:
- block_output: float32 [12, 2048, 576], P('fsdp', 'ctx')
- input_gradient: float32 [12, 2048, 576], P('fsdp', 'ctx')
- query_next: float32 [576, 576], P('fsdp', 'ctx')
- key_next: float32 [576, 192], P('fsdp', 'ctx')
- value_next: float32 [576, 192], P('fsdp', 'ctx')
- output_next: float32 [576, 576], P('fsdp', 'ctx')
- gate_next: float32 [576, 1536], P('fsdp', 'ctx')
- up_next: float32 [576, 1536], P('fsdp', 'ctx')
- down_next: float32 [1536, 576], P('fsdp', 'ctx')
- gains_next: float32 [576, 2], P('fsdp')
- query_first_next: float32 [576, 576], P('fsdp', 'ctx')
- key_first_next: float32 [576, 192], P('fsdp', 'ctx')
- value_first_next: float32 [576, 192], P('fsdp', 'ctx')
- output_first_next: float32 [576, 576], P('fsdp', 'ctx')
- gate_first_next: float32 [576, 1536], P('fsdp', 'ctx')
- up_first_next: float32 [576, 1536], P('fsdp', 'ctx')
- down_first_next: float32 [1536, 576], P('fsdp', 'ctx')
- gains_first_next: float32 [576, 2], P('fsdp')
- query_second_next: float32 [576, 576], P('fsdp', 'ctx')
- key_second_next: float32 [576, 192], P('fsdp', 'ctx')
- value_second_next: float32 [576, 192], P('fsdp', 'ctx')
- output_second_next: float32 [576, 576], P('fsdp', 'ctx')
- gate_second_next: float32 [576, 1536], P('fsdp', 'ctx')
- up_second_next: float32 [576, 1536], P('fsdp', 'ctx')
- down_second_next: float32 [1536, 576], P('fsdp', 'ctx')
- gains_second_next: float32 [576, 2], P('fsdp')
Inputs may be any that keep to these rules, and one draw needn't show every extreme that they name: `pair_order`: each row is a permutation of 0 to 15.
All inputs are finite; a program needn't handle non-finite values.
Results may differ from a plain program's by a relative error of at most 0.024.
Values may be sent and summed in bfloat16 or wider, within the bound.
No kernel may reach another device: no remote copies, remote signals or barrier semaphores. Data moves between devices by JAX's collectives and lax.ppermute only.
A program may use at most 192 MiB of HBM per device.

v0:
```python
import jax
import jax.numpy as jnp
from jax import lax
from jax.sharding import PartitionSpec as P

MODEL_WIDTH = 576
FF = 1536
HEADS = 9
KV_HEADS = 3
HEAD_DIM = 64
STEP = 10


NORM_EPS = 1e-05
ROPE_BASE = 100000.0
BETA_ONE = 0.9
BETA_TWO = 0.95
ADAM_EPS = 1e-08
DECAY = 0.1
GAIN_RATE = 0.5
MASKED = -1e30


def rotate(field, cosine, sine):
    half_dim = field.shape[-1] // 2
    first_half = field[..., :half_dim]
    second_half = field[..., half_dim:]
    return jnp.concatenate(
        [first_half * cosine - second_half * sine, second_half * cosine + first_half * sine],
        axis=-1,
    )


def tables(places):
    half_dim = HEAD_DIM // 2
    inverse = ROPE_BASE ** (-jnp.arange(half_dim, dtype=jnp.float32) * 2.0 / HEAD_DIM)
    angle = places.astype(jnp.float32)[..., None] * inverse
    return (jnp.cos(angle), jnp.sin(angle))


def order_positions(pair_order, half_rows, devices_ctx):
    within = jnp.arange(half_rows, dtype=jnp.int32)
    early = pair_order[:, :, None] * half_rows + within[None, None, :]
    late = (2 * devices_ctx - 1 - pair_order)[:, :, None] * half_rows + within[None, None, :]
    return jnp.concatenate([early, late], axis=2).reshape(
        pair_order.shape[0], devices_ctx * 2 * half_rows
    )


def norm_back(grad_normed, normed_hat, inv_root, gain):
    scaled = grad_normed * gain
    return inv_root * (scaled - normed_hat * jnp.mean(scaled * normed_hat, axis=-1, keepdims=True))


def masked_scores(query_five, keys_four, query_places, key_places, factor):
    scores = (
        jnp.einsum("srjgd,stjd->sjgrt", query_five, keys_four, preferred_element_type=jnp.float32)
        * factor
    )
    allowed = key_places[:, None, :] <= query_places[:, :, None]
    return jnp.where(allowed[:, None, None], scores, MASKED)


def score_terms(
    query_five,
    grad_five,
    keys_four,
    values_four,
    query_places,
    key_places,
    log_total,
    row_delta,
    factor,
):
    scores = masked_scores(query_five, keys_four, query_places, key_places, factor)
    prob_full = jnp.exp(scores - log_total[..., None])
    grad_prob = jnp.einsum(
        "srjgd,stjd->sjgrt", grad_five, values_four, preferred_element_type=jnp.float32
    )
    grad_scores = (prob_full * (grad_prob - row_delta[..., None])).astype(jnp.bfloat16)
    return (grad_scores, prob_full.astype(jnp.bfloat16))


def adam_update(weight, first, second, grad, rate, decay):
    first_next = BETA_ONE * first + (1.0 - BETA_ONE) * grad
    second_next = BETA_TWO * second + (1.0 - BETA_TWO) * grad * grad
    first_fix = first_next / (1.0 - BETA_ONE**STEP)
    second_fix = second_next / (1.0 - BETA_TWO**STEP)
    update = first_fix / (jnp.sqrt(second_fix) + ADAM_EPS) + decay * weight
    return (weight - rate * update, first_next, second_next)


def gather_columns(query_part, key_part, value_part, output_part, gate_part, up_part, down_part):
    return (
        lax.all_gather(query_part, "ctx", axis=1, tiled=True),
        lax.all_gather(key_part, "ctx", axis=1, tiled=True),
        lax.all_gather(value_part, "ctx", axis=1, tiled=True),
        lax.all_gather(output_part, "ctx", axis=1, tiled=True),
        lax.all_gather(gate_part, "ctx", axis=1, tiled=True),
        lax.all_gather(up_part, "ctx", axis=1, tiled=True),
        lax.all_gather(down_part, "ctx", axis=1, tiled=True),
    )


def gather_rows(
    query_part, key_part, value_part, output_part, gate_part, up_part, down_part, gains_part
):
    return (
        lax.all_gather(query_part, "fsdp", axis=0, tiled=True),
        lax.all_gather(key_part, "fsdp", axis=0, tiled=True),
        lax.all_gather(value_part, "fsdp", axis=0, tiled=True),
        lax.all_gather(output_part, "fsdp", axis=0, tiled=True),
        lax.all_gather(gate_part, "fsdp", axis=0, tiled=True),
        lax.all_gather(up_part, "fsdp", axis=0, tiled=True),
        lax.all_gather(down_part, "fsdp", axis=0, tiled=True),
        lax.all_gather(gains_part, "fsdp", axis=0, tiled=True),
    )


def sum_columns(query_part, key_part, value_part, output_part, gate_part, up_part, down_part):
    return (
        lax.psum_scatter(
            query_part.astype(jnp.bfloat16), "ctx", scatter_dimension=1, tiled=True
        ).astype(jnp.float32),
        lax.psum_scatter(
            key_part.astype(jnp.bfloat16), "ctx", scatter_dimension=1, tiled=True
        ).astype(jnp.float32),
        lax.psum_scatter(
            value_part.astype(jnp.bfloat16), "ctx", scatter_dimension=1, tiled=True
        ).astype(jnp.float32),
        lax.psum_scatter(
            output_part.astype(jnp.bfloat16), "ctx", scatter_dimension=1, tiled=True
        ).astype(jnp.float32),
        lax.psum_scatter(
            gate_part.astype(jnp.bfloat16), "ctx", scatter_dimension=1, tiled=True
        ).astype(jnp.float32),
        lax.psum_scatter(
            up_part.astype(jnp.bfloat16), "ctx", scatter_dimension=1, tiled=True
        ).astype(jnp.float32),
        lax.psum_scatter(
            down_part.astype(jnp.bfloat16), "ctx", scatter_dimension=1, tiled=True
        ).astype(jnp.float32),
    )


def sum_rows(
    query_part, key_part, value_part, output_part, gate_part, up_part, down_part, gains_part
):
    return (
        lax.psum_scatter(
            query_part.astype(jnp.bfloat16), "fsdp", scatter_dimension=0, tiled=True
        ).astype(jnp.float32),
        lax.psum_scatter(
            key_part.astype(jnp.bfloat16), "fsdp", scatter_dimension=0, tiled=True
        ).astype(jnp.float32),
        lax.psum_scatter(
            value_part.astype(jnp.bfloat16), "fsdp", scatter_dimension=0, tiled=True
        ).astype(jnp.float32),
        lax.psum_scatter(
            output_part.astype(jnp.bfloat16), "fsdp", scatter_dimension=0, tiled=True
        ).astype(jnp.float32),
        lax.psum_scatter(
            gate_part.astype(jnp.bfloat16), "fsdp", scatter_dimension=0, tiled=True
        ).astype(jnp.float32),
        lax.psum_scatter(
            up_part.astype(jnp.bfloat16), "fsdp", scatter_dimension=0, tiled=True
        ).astype(jnp.float32),
        lax.psum_scatter(
            down_part.astype(jnp.bfloat16), "fsdp", scatter_dimension=0, tiled=True
        ).astype(jnp.float32),
        lax.psum_scatter(
            gains_part.astype(jnp.bfloat16), "fsdp", scatter_dimension=0, tiled=True
        ).astype(jnp.float32),
    )


def body(
    tokens,
    cotangent,
    pair_order,
    query_weight,
    key_master_weight,
    value_master_weight,
    output_weight,
    gate_weight,
    up_weight,
    down_weight,
    norm_gains,
    query_first,
    key_first_moment,
    value_first_moment,
    output_first,
    gate_first,
    up_first,
    down_first,
    gains_first,
    query_second,
    key_second_moment,
    value_second_moment,
    output_second,
    gate_second,
    up_second,
    down_second,
    gains_second,
):
    masters = (
        query_weight,
        key_master_weight,
        value_master_weight,
        output_weight,
        gate_weight,
        up_weight,
        down_weight,
    )
    lowered = tuple((matrix.astype(jnp.bfloat16) for matrix in masters))
    gains_low = norm_gains.astype(jnp.bfloat16)
    row_full = gather_rows(*lowered, gains_low)
    gathered = tuple(gather_columns(*row_full[:7])) + (row_full[7],)
    full_query, full_key, full_value, full_output, full_gate, full_up, full_down, full_gains = (
        gathered
    )
    seqs_here = tokens.shape[0]
    rows_here = tokens.shape[1]
    devices_ctx = lax.axis_size("ctx")
    seq_length = rows_here * devices_ctx
    my_index = lax.axis_index("ctx")
    places_all = order_positions(pair_order, rows_here // 2, devices_ctx)
    places_own = lax.dynamic_slice_in_dim(places_all, my_index * rows_here, rows_here, 1)
    group = HEADS // KV_HEADS
    key_width = KV_HEADS * HEAD_DIM
    query_width = HEADS * HEAD_DIM
    factor = HEAD_DIM ** (-0.5)
    block_rows = min(512, seq_length)
    block_count = seq_length // block_rows
    block_range = jnp.arange(block_count)
    cosine, sine = tables(places_own)
    cosine_four = cosine[:, :, None, :]
    sine_four = sine[:, :, None, :]
    inputs = tokens.astype(jnp.float32)
    inv_one = lax.rsqrt(jnp.mean(inputs * inputs, axis=-1, keepdims=True) + NORM_EPS)
    hat_one = inputs * inv_one
    gain_one = full_gains[:, 0].astype(jnp.float32)
    gain_two = full_gains[:, 1].astype(jnp.float32)
    normed_one = (hat_one * gain_one).astype(jnp.bfloat16)
    query_raw = jnp.dot(normed_one, full_query, preferred_element_type=jnp.float32)
    key_raw = jnp.dot(normed_one, full_key, preferred_element_type=jnp.float32)
    value_raw = jnp.dot(normed_one, full_value, preferred_element_type=jnp.float32)
    query_rot = rotate(
        query_raw.reshape(seqs_here, rows_here, HEADS, HEAD_DIM), cosine_four, sine_four
    ).astype(jnp.bfloat16)
    query_five = query_rot.reshape(seqs_here, rows_here, KV_HEADS, group, HEAD_DIM)
    key_four = rotate(
        key_raw.reshape(seqs_here, rows_here, KV_HEADS, HEAD_DIM), cosine_four, sine_four
    ).astype(jnp.bfloat16)
    value_low = value_raw.astype(jnp.bfloat16)
    joined = jnp.concatenate(
        [key_four.reshape(seqs_here, rows_here, key_width), value_low], axis=-1
    )
    kv_all = lax.all_gather(joined, "ctx", axis=1, tiled=True)

    def key_block(block_index):
        begin_row = block_index * block_rows
        piece_rows = lax.dynamic_slice_in_dim(kv_all, begin_row, block_rows, 1)
        keys_four = piece_rows[..., :key_width].reshape(seqs_here, block_rows, KV_HEADS, HEAD_DIM)
        values_four = piece_rows[..., key_width:].reshape(seqs_here, block_rows, KV_HEADS, HEAD_DIM)
        key_places = lax.dynamic_slice_in_dim(places_all, begin_row, block_rows, 1)
        return (keys_four, values_four, key_places)

    def stats_step(carried, block_index):
        row_top, row_total = carried
        keys_four, values_four, key_places = key_block(block_index)
        scores = masked_scores(query_five, keys_four, places_own, key_places, factor)
        new_top = jnp.maximum(row_top, jnp.max(scores, axis=-1))
        row_total = row_total * jnp.exp(row_top - new_top) + jnp.sum(
            jnp.exp(scores - new_top[..., None]), axis=-1
        )
        return ((new_top, row_total), None)

    stat_shape = (seqs_here, KV_HEADS, group, rows_here)
    stat_init = (jnp.full(stat_shape, MASKED, jnp.float32), jnp.zeros(stat_shape, jnp.float32))
    (row_top, row_total), unused = lax.scan(stats_step, stat_init, block_range)
    log_total = row_top + jnp.log(row_total)

    def output_step(accum, block_index):
        keys_four, values_four, key_places = key_block(block_index)
        scores = masked_scores(query_five, keys_four, places_own, key_places, factor)
        prob_low = jnp.exp(scores - log_total[..., None]).astype(jnp.bfloat16)
        return (
            accum
            + jnp.einsum(
                "sjgrt,stjd->sjgrd", prob_low, values_four, preferred_element_type=jnp.float32
            ),
            None,
        )

    heads_zero = jnp.zeros((seqs_here, KV_HEADS, group, rows_here, HEAD_DIM), jnp.float32)
    attended, unused = lax.scan(output_step, heads_zero, block_range)
    attn_low = (
        attended.transpose(0, 3, 1, 2, 4)
        .reshape(seqs_here, rows_here, query_width)
        .astype(jnp.bfloat16)
    )
    resid_one = inputs + jnp.dot(attn_low, full_output, preferred_element_type=jnp.float32)
    inv_two = lax.rsqrt(jnp.mean(resid_one * resid_one, axis=-1, keepdims=True) + NORM_EPS)
    hat_two = resid_one * inv_two
    normed_two = (hat_two * gain_two).astype(jnp.bfloat16)
    gate_raw = jnp.dot(normed_two, full_gate, preferred_element_type=jnp.float32)
    up_raw = jnp.dot(normed_two, full_up, preferred_element_type=jnp.float32)
    gate_sig = jax.nn.sigmoid(gate_raw)
    gate_act = gate_raw * gate_sig
    hidden_low = (gate_act * up_raw).astype(jnp.bfloat16)
    block_output = resid_one + jnp.dot(hidden_low, full_down, preferred_element_type=jnp.float32)
    grad_out = cotangent.astype(jnp.float32)
    down_grad = jnp.einsum("srf,srd->fd", hidden_low, cotangent, preferred_element_type=jnp.float32)
    grad_hidden = jnp.einsum(
        "srd,fd->srf", cotangent, full_down, preferred_element_type=jnp.float32
    )
    gate_grad_low = (
        grad_hidden * up_raw * (gate_sig * (1.0 + gate_raw * (1.0 - gate_sig)))
    ).astype(jnp.bfloat16)
    up_grad_low = (grad_hidden * gate_act).astype(jnp.bfloat16)
    gate_grad = jnp.einsum(
        "srd,srf->df", normed_two, gate_grad_low, preferred_element_type=jnp.float32
    )
    up_grad = jnp.einsum("srd,srf->df", normed_two, up_grad_low, preferred_element_type=jnp.float32)
    grad_normed_two = jnp.einsum(
        "srf,df->srd", gate_grad_low, full_gate, preferred_element_type=jnp.float32
    ) + jnp.einsum("srf,df->srd", up_grad_low, full_up, preferred_element_type=jnp.float32)
    gain_two_grad = jnp.sum(grad_normed_two * hat_two, axis=(0, 1))
    grad_resid = grad_out + norm_back(grad_normed_two, hat_two, inv_two, gain_two)
    grad_attn_low = grad_resid.astype(jnp.bfloat16)
    output_grad = jnp.einsum(
        "srh,srd->hd", attn_low, grad_attn_low, preferred_element_type=jnp.float32
    )
    grad_heads = jnp.einsum(
        "srd,hd->srh", grad_attn_low, full_output, preferred_element_type=jnp.float32
    ).astype(jnp.bfloat16)
    grad_five = grad_heads.reshape(seqs_here, rows_here, KV_HEADS, group, HEAD_DIM)
    row_delta = jnp.einsum(
        "srjgd,sjgrd->sjgr", grad_five, attended, preferred_element_type=jnp.float32
    )
    query_zero = jnp.zeros((seqs_here, rows_here, KV_HEADS, group, HEAD_DIM), jnp.float32)

    def joint_step(carried, block_index):
        grad_query, grad_buffer = carried
        keys_four, values_four, key_places = key_block(block_index)
        grad_scores, prob_low = score_terms(
            query_five,
            grad_five,
            keys_four,
            values_four,
            places_own,
            key_places,
            log_total,
            row_delta,
            factor,
        )
        grad_query = (
            grad_query
            + jnp.einsum(
                "sjgrt,stjd->srjgd", grad_scores, keys_four, preferred_element_type=jnp.float32
            )
            * factor
        )
        grad_keys = (
            jnp.einsum(
                "sjgrt,srjgd->stjd", grad_scores, query_five, preferred_element_type=jnp.float32
            )
            * factor
        )
        grad_values = jnp.einsum(
            "sjgrt,srjgd->stjd", prob_low, grad_five, preferred_element_type=jnp.float32
        )
        block_grads = jnp.concatenate(
            [
                grad_keys.reshape(seqs_here, block_rows, key_width),
                grad_values.reshape(seqs_here, block_rows, key_width),
            ],
            axis=-1,
        )
        grad_buffer = lax.dynamic_update_slice_in_dim(
            grad_buffer, block_grads, block_index * block_rows, 1
        )
        return ((grad_query, grad_buffer), None)

    buffer_zero = jnp.zeros((seqs_here, seq_length, 2 * key_width), jnp.float32)
    (grad_query_rot, grad_buffer), unused = lax.scan(
        joint_step, (query_zero, buffer_zero), block_range
    )
    grad_own = lax.psum_scatter(
        grad_buffer.astype(jnp.bfloat16), "ctx", scatter_dimension=1, tiled=True
    ).astype(jnp.float32)
    grad_key_rot = grad_own[..., :key_width].reshape(seqs_here, rows_here, KV_HEADS, HEAD_DIM)
    grad_value = grad_own[..., key_width:].reshape(seqs_here, rows_here, KV_HEADS, HEAD_DIM)
    grad_query_low = (
        rotate(
            grad_query_rot.reshape(seqs_here, rows_here, HEADS, HEAD_DIM), cosine_four, -sine_four
        )
        .astype(jnp.bfloat16)
        .reshape(seqs_here, rows_here, query_width)
    )
    grad_key_low = (
        rotate(grad_key_rot, cosine_four, -sine_four)
        .astype(jnp.bfloat16)
        .reshape(seqs_here, rows_here, key_width)
    )
    grad_value_low = grad_value.astype(jnp.bfloat16).reshape(seqs_here, rows_here, key_width)
    query_grad = jnp.einsum(
        "srd,srh->dh", normed_one, grad_query_low, preferred_element_type=jnp.float32
    )
    key_grad = jnp.einsum(
        "srd,srh->dh", normed_one, grad_key_low, preferred_element_type=jnp.float32
    )
    value_grad = jnp.einsum(
        "srd,srh->dh", normed_one, grad_value_low, preferred_element_type=jnp.float32
    )
    grad_normed_one = (
        jnp.einsum("srh,dh->srd", grad_query_low, full_query, preferred_element_type=jnp.float32)
        + jnp.einsum("srh,dh->srd", grad_key_low, full_key, preferred_element_type=jnp.float32)
        + jnp.einsum("srh,dh->srd", grad_value_low, full_value, preferred_element_type=jnp.float32)
    )
    gain_one_grad = jnp.sum(grad_normed_one * hat_one, axis=(0, 1))
    input_gradient = grad_resid + norm_back(grad_normed_one, hat_one, inv_one, gain_one)
    gains_grad = jnp.stack([gain_one_grad, gain_two_grad], axis=1)
    local_grads = (query_grad, key_grad, value_grad, output_grad, gate_grad, up_grad, down_grad)
    column_sums = sum_columns(*local_grads)
    row_sums = sum_rows(*column_sums, gains_grad)
    reduced = row_sums[:7]
    gains_part = row_sums[7]
    gains_total = lax.psum(gains_part, "ctx")
    rates = (
        (MODEL_WIDTH // 4) ** (-0.5),
        MODEL_WIDTH ** (-0.5),
        MODEL_WIDTH ** (-0.5),
        (MODEL_WIDTH // 32) ** (-0.5),
        MODEL_WIDTH ** (-0.5),
        MODEL_WIDTH ** (-0.5),
        (FF // 2) ** (-0.5),
    )
    firsts = (
        query_first,
        key_first_moment,
        value_first_moment,
        output_first,
        gate_first,
        up_first,
        down_first,
    )
    seconds = (
        query_second,
        key_second_moment,
        value_second_moment,
        output_second,
        gate_second,
        up_second,
        down_second,
    )
    results = [
        adam_update(
            masters[member], firsts[member], seconds[member], reduced[member], rates[member], DECAY
        )
        for member in range(7)
    ]
    results.append(adam_update(norm_gains, gains_first, gains_second, gains_total, GAIN_RATE, 0.0))
    new_weights = [result[0] for result in results]
    new_firsts = [result[1] for result in results]
    new_seconds = [result[2] for result in results]
    return tuple([block_output, input_gradient] + new_weights + new_firsts + new_seconds)


def solution(mesh):
    placed = (
        P("fsdp", "ctx", None),
        P("fsdp", "ctx", None),
        P("fsdp", None),
        P("fsdp", "ctx"),
        P("fsdp", "ctx"),
        P("fsdp", "ctx"),
        P("fsdp", "ctx"),
        P("fsdp", "ctx"),
        P("fsdp", "ctx"),
        P("fsdp", "ctx"),
        P("fsdp", None),
        P("fsdp", "ctx"),
        P("fsdp", "ctx"),
        P("fsdp", "ctx"),
        P("fsdp", "ctx"),
        P("fsdp", "ctx"),
        P("fsdp", "ctx"),
        P("fsdp", "ctx"),
        P("fsdp", None),
        P("fsdp", "ctx"),
        P("fsdp", "ctx"),
        P("fsdp", "ctx"),
        P("fsdp", "ctx"),
        P("fsdp", "ctx"),
        P("fsdp", "ctx"),
        P("fsdp", "ctx"),
        P("fsdp", None),
    )
    return jax.shard_map(
        body,
        mesh=mesh,
        in_specs=placed,
        out_specs=(
            P("fsdp", "ctx", None),
            P("fsdp", "ctx", None),
            P("fsdp", "ctx"),
            P("fsdp", "ctx"),
            P("fsdp", "ctx"),
            P("fsdp", "ctx"),
            P("fsdp", "ctx"),
            P("fsdp", "ctx"),
            P("fsdp", "ctx"),
            P("fsdp", None),
            P("fsdp", "ctx"),
            P("fsdp", "ctx"),
            P("fsdp", "ctx"),
            P("fsdp", "ctx"),
            P("fsdp", "ctx"),
            P("fsdp", "ctx"),
            P("fsdp", "ctx"),
            P("fsdp", None),
            P("fsdp", "ctx"),
            P("fsdp", "ctx"),
            P("fsdp", "ctx"),
            P("fsdp", "ctx"),
            P("fsdp", "ctx"),
            P("fsdp", "ctx"),
            P("fsdp", "ctx"),
            P("fsdp", None),
        ),
        check_vma=False,
    )
```

profile of v0, /device:TPU:0, one launch (start us, length us, event | category | flops | bytes accessed | tf_op | source)
XLA Modules:
  0.0 940.6 jit_solution(16673971919404382627)
XLA Ops:
  8.2 5.9 all_gather.62
  30.7 23.5 %all-gather.4 = bf16[16,12,576]{2,1,0:T(8,128)(2,1)S(1)} all-gather(bf16[1,12,576]{2,1,0:T(8,128)(2,1)S(1)} %bitcast.335), channel_id=1, replica_groups=mesh['ctx'=16,'fsdp'=2] {'ctx'}, dimensions={0}, use_global_device_ids=true | all-gather | bytes 235008 | tf_op jit(solution)/shard_map/all_gather | solution.py:97
  54.3 18.3 %all-gather.2 = bf16[16,12,576]{2,1,0:T(8,128)(2,1)S(1)} all-gather(bf16[1,12,576]{2,1,0:T(8,128)(2,1)S(1)} %bitcast.334), channel_id=1, replica_groups=mesh['ctx'=16,'fsdp'=2] {'ctx'}, dimensions={0}, use_global_device_ids=true | all-gather | bytes 235008 | tf_op jit(solution)/shard_map/all_gather | solution.py:96
  76.3 5.2 all_gather.60
  97.8 23.8 %all-gather.8 = bf16[16,36,576]{2,1,0:T(8,128)(2,1)S(1)} all-gather(bf16[1,36,576]{2,1,0:T(8,128)(2,1)S(1)} %bitcast.333), channel_id=1, replica_groups=mesh['ctx'=16,'fsdp'=2] {'ctx'}, dimensions={0}, use_global_device_ids=true | all-gather | bytes 705024 | tf_op jit(solution)/shard_map/all_gather | solution.py:98
  122.8 24.6 %all-gather.6 = bf16[16,36,576]{2,1,0:T(8,128)(2,1)S(1)} all-gather(bf16[1,36,576]{2,1,0:T(8,128)(2,1)S(1)} %bitcast.332), channel_id=1, replica_groups=mesh['ctx'=16,'fsdp'=2] {'ctx'}, dimensions={0}, use_global_device_ids=true | all-gather | bytes 705024 | tf_op jit(solution)/shard_map/all_gather | solution.py:95
  156.0 13.9 %all-gather.15.cloned.1.call-done = bf16[6,2048,384]{1,2,0:T(8,128)(2,1)} async-done(((bf16[6,128,384]{1,2,0:T(8,128)(2,1)}), bf16[6,2048,384]{1,2,0:T(8,128)(2,1)}) %all-gather.15.cloned.1.call-update) | async-done | bytes 9437200 | tf_op jit(solution)/shard_map/all_gather | solution.py:259
  169.9 79.5 %while.37 = (s32[]{:T(128)}, f32[6,3,3,128]{3,2,1,0:T(4,128)}, f32[6,3,3,128]{3,2,1,0:T(4,128)}, s32[4]{0:T(128)S(1)}, s32[6,2048]{1,0:T(8,128)}, /*index=5*/s32...) while((s32[]{:T(128)}, f32[6,3,3,128]{3,2,1,0:T(4,128)}, ...), condition=%wide.region_4.5_spmd.clone, body=%wide.region_1.4_spmd.clone.sunk | while | flops 478185216 | bytes 34646300 | solution.py:281
  173.8 6.3 fusion.165
  180.2 8.9 exponential_reduce_fusion.2
  193.7 6.2 fusion.165
  200.0 8.9 exponential_reduce_fusion.2
  213.5 6.2 fusion.165
  219.8 9.0 exponential_reduce_fusion.2
  233.4 6.4 fusion.165
  239.8 8.9 exponential_reduce_fusion.2
  250.2 48.4 %while.38 = (s32[]{:T(128)}, f32[6,3,3,128,64]{3,4,2,1,0:T(8,128)}, s32[4]{0:T(128)S(1)}, s32[6,2048]{1,0:T(8,128)}, s32[6,128]{1,0:T(8,128)S(1)}, /*index=5*/bf...) while((s32[]{:T(128)}, f32[6,3,3,128,64]{3,4,2,1,0:T(8,128)}, ...), condition=%wide.region_6.7_spmd.clone, body=%wide.region_5.6_spmd.clone.sunk | while | flops 921403392 | bytes 12355809 | solution.py:297
  255.6 6.5 select_add_fusion.2
  267.2 7.1 select_add_fusion.2
  279.4 7.1 select_add_fusion.2
  291.6 7.1 select_add_fusion.2
  303.0 5.7 fusion.30
  308.7 8.7 multiply_convert_fusion.1
  339.7 42.6 %reduce-scatter.38.cloned.1.call-done = bf16[576,96]{0,1:T(8,128)(2,1)} async-done(((bf16[576,1536]{0,1:T(8,128)(2,1)}), bf16[576,96]{0,1:T(8,128)(2,1)}) %reduce-scatter.38.cloned.1.call-update) | async-done | bytes 110608 | tf_op jit(solution)/shard_map/reduce_scatter | solution.py:134
  386.5 59.6 %reduce-scatter.40.cloned.1.call-done = bf16[576,96]{0,1:T(8,128)(2,1)} async-done(((bf16[576,1536]{0,1:T(8,128)(2,1)}), bf16[576,96]{0,1:T(8,128)(2,1)}) %reduce-scatter.40.cloned.1.call-update) | async-done | bytes 110608 | tf_op jit(solution)/shard_map/reduce_scatter | solution.py:137
  452.7 139.2 %while.39 = (s32[]{:T(128)}, f32[6,128,3,3,64]{1,4,3,2,0:T(8,128)S(1)}, bf16[6,2048,384]{1,2,0:T(8,128)(2,1)}, s32[4]{0:T(128)S(1)}, bf16[6,2048,384]{1,2,0:T(8,...) while((s32[]{:T(128)}, ...), condition=%wide.region_10.11_spmd.clone, body=%wide.region_9.10_spmd.clone.sunk | while | flops 2307932160 | bytes 87638328 | solution.py:387
  458.3 6.2 fusion.180
  464.5 8.6 fusion.182
  473.1 8.9 fusion.181
  493.1 6.2 fusion.180
  499.3 8.5 fusion.182
  507.8 8.9 fusion.181
  527.9 6.2 fusion.180
  534.0 8.5 fusion.182
  542.6 8.9 fusion.181
  562.6 6.2 fusion.180
  568.8 8.5 fusion.182
  577.3 8.9 fusion.181
  591.9 15.8 %copy.158 = bf16[6,2048,384]{2,0,1:T(8,128)(2,1)} copy(bf16[6,2048,384]{1,2,0:T(8,128)(2,1)} %get-tuple-element.173) | data formatting | bytes 18874368
  607.7 10.5 %copy.177 = bf16[256,8,6,384]{3,1,2,0:T(8,128)(2,1)} copy(bf16[256,8,6,384]{3,2,1,0:T(8,128)(2,1)} %bitcast.308) | data formatting | bytes 18874368
  654.8 73.9 %reduce-scatter.44.cloned.1.call-done = bf16[128,2304]{1,0:T(8,128)(2,1)} async-done(((bf16[2048,2304]{1,0:T(8,128)(2,1)}), bf16[128,2304]{1,0:T(8,128)(2,1)}) %reduce-scatter.44.cloned.1.call-update) | async-done | bytes 589840
  739.5 52.1 %fusion.80 = (bf16[576,48]{0,1:T(8,128)(2,1)S(1)}, bf16[576,16]{0,1:T(8,128)(2,1)S(1)}, bf16[576,16]{0,1:T(8,128)(2,1)S(1)}, bf16[576,48]{0,1:T(8,128)(2,1)S(1)}, bf16[1536,40]{0,1:T(8,128)(2,1)S(1)}) fusion(bf16[576,576]{0,1:T(8,128)(2,1)} %bitcast_convert_fusion.4, bf16[576,192]{0,1:T(8,128)(2,1)} %fusion.47, bf16[576,192]{0,1:T(8,128)(2,1)} %fusion.48, ...), kind=kCustom, calls=%all-reduce-scatter.5 | all-reduce-scatter fusion | flops 2162691 | bytes 3809792
  805.3 7.9 collective-permute-start.10
  818.2 31.8 %psum.7 = f32[288,2]{0,1:T(2,128)S(1)} all-reduce(bf16[288,2]{0,1:T(2,128)(2,1)S(1)} %copy.173), channel_id=1, replica_groups=mesh['ctx'=16,'fsdp'=2] {'ctx'}, use_global_device_ids=true, to_apply=%region_30.31 | all-reduce | flops 576 | bytes 3456 | tf_op jit(solution)/shard_map/psum | solution.py:430
  862.0 8.1 collective-permute-start.14
  876.6 5.3 reduce-scatter.48.cloned.1.call-done
  908.3 11.0 %reduce-scatter.52.cloned.1.call-done = bf16[288,36]{1,0:T(8,128)(2,1)} async-done(((bf16[576,36]{1,0:T(8,128)(2,1)}), bf16[288,36]{1,0:T(8,128)(2,1)}) %reduce-scatter.52.cloned.1.call-update) | async-done | bytes 20752
  921.0 11.2 %reduce-scatter.42.cloned.1.call-done = bf16[768,36]{0,1:T(8,128)(2,1)} async-done(((bf16[1536,36]{0,1:T(8,128)(2,1)}), bf16[768,36]{0,1:T(8,128)(2,1)}) %reduce-scatter.42.cloned.1.call-update) | async-done | bytes 55312 | tf_op jit(solution)/shard_map/reduce_scatter | solution.py:168
  (488 shorter events, 272.6 us)
Async XLA Ops:
  7.2 65.6 %copy-start.2 = (bf16[6,128,576]{1,2,0:T(8,128)(2,1)S(1)}, bf16[6,128,576]{1,2,0:T(8,128)(2,1)}, u32[]{:S(2)}) copy-start(bf16[6,128,576]{1,2,0:T(8,128)(2,1)} %param.33) | copy-start | bytes 2654212
  7.2 142.0 %all-gather.21.cloned.1.call-start = ((), (), s32[]{:S(2)}) async-start(), calls=%async_computation.17 | async-start | bytes 2088960 | tf_op jit(solution)/shard_map/all_gather | solution.py:101
  14.2 155.7 %all-gather.15.cloned.1.call-start = ((), (), s32[]{:S(2)}) async-start(), calls=%async_computation.11 | async-start | bytes 10027008 | tf_op jit(solution)/shard_map/all_gather | solution.py:259
  30.7 43.9 %copy-start.23 = (s32[1,6,16,128]{3,1,2,0:T(8,128)}, s32[1,6,16,128]{3,1,2,0:T(8,128)S(1)}, u32[]{:S(2)}) copy-start(s32[1,6,16,128]{3,1,2,0:T(8,128)S(1)} %copy.179) | copy-start | bytes 147460
  72.8 74.9 %copy-start.66 = (f32[576]{0:T(1024)}, f32[576]{0:T(1024)S(1)}, u32[]{:S(2)}) copy-start(f32[576]{0:T(1024)S(1)} %get-tuple-element.363) | copy-start | bytes 6916
  73.1 74.7 %copy-start.68 = (f32[6,128]{1,0:T(8,128)}, f32[6,128]{1,0:T(8,128)S(1)}, u32[]{:S(2)}) copy-start(f32[6,128]{1,0:T(8,128)S(1)} %add_rsqrt_fusion.1) | copy-start | bytes 9220
  74.1 74.6 %copy-start.20 = (f32[6,128,32]{1,2,0:T(8,128)}, f32[6,128,32]{1,2,0:T(8,128)S(1)}, u32[]{:S(2)}) copy-start(f32[6,128,32]{1,2,0:T(8,128)S(1)} %get-tuple-element.475) | copy-start | bytes 294916
  76.3 226.7 %all-gather.19.cloned.1.call-start = ((), (), s32[]{:S(2)}) async-start(), calls=%async_computation.13 | async-start | bytes 2088960 | tf_op jit(solution)/shard_map/all_gather | solution.py:100
  82.3 226.4 %all-gather.17.cloned.1.call-start = ((), (), s32[]{:S(2)}) async-start(), calls=%async_computation.12 | async-start | bytes 2088960 | tf_op jit(solution)/shard_map/all_gather | solution.py:99
  88.3 294.1 %reduce-scatter.38.cloned.1.call-start = ((), (), s32[]{:S(2)}) async-start(), calls=%async_computation.14 | async-start | bytes 2088960 | tf_op jit(solution)/shard_map/reduce_scatter | solution.py:134
  322.3 123.8 %reduce-scatter.40.cloned.1.call-start = ((), (), s32[]{:S(2)}) async-start(), calls=%async_computation.15 | async-start | bytes 2088960 | tf_op jit(solution)/shard_map/reduce_scatter | solution.py:137
  327.8 312.8 %reduce-scatter.54.cloned.1.call-start = ((), (), s32[]{:S(2)}) async-start(), calls=%async_computation.23 | async-start | bytes 221184
  384.0 261.7 %reduce-scatter.56.cloned.1.call-start = ((), (), s32[]{:S(2)}) async-start(), calls=%async_computation.24 | async-start | bytes 221184
  447.8 280.9 %reduce-scatter.44.cloned.1.call-start = ((), (), s32[]{:S(2)}) async-start(), calls=%async_computation.18 | async-start | bytes 10027008
  618.3 198.9 %reduce-scatter.58.cloned.1.call-start = ((), (), s32[]{:S(2)}) async-start(), calls=%async_computation.25 | async-start | bytes 221184
  739.5 54.4 %copy-start.27 = (bf16[192,576,1]{1,0,2:T(8,128)(2,1)S(1)}, bf16[192,576,1]{1,0,2:T(8,128)(2,1)}, u32[]{:S(2)}) copy-start(bf16[192,576,1]{1,0,2:T(8,128)(2,1)} %copy-done.26) | copy-start | bytes 663556
  791.6 59.0 %collective-permute-start.11 = (bf16[576,12]{0,1:T(8,128)(2,1)S(1)}, bf16[576,12]{0,1:T(8,128)(2,1)S(1)}, u32[]{:S(2)}, u32[]{:S(2)}) collective-permute-start(bf16[576,12]{0,1:T(8,128)(2,1)S(1)} %slice.84), channel_id=1, source_target_pairs={{0,8},{2,10},{4,12},{6,14},{8,16},{10,18},{12,20},{14,22},{16,24},... | collective-permute-start | bytes 41480
  798.8 76.1 %reduce-scatter.50.cloned.1.call-start = ((), (), s32[]{:S(2)}) async-start(), calls=%async_computation.21 | async-start | bytes 221184
  798.9 51.1 %copy-start.75 = (f32[288,2]{0,1:T(2,128)S(1)}, f32[288,2]{0,1:T(2,128)}, u32[]{:S(2)}) copy-start(f32[288,2]{0,1:T(2,128)} %param.43) | copy-start | bytes 6916
  798.9 51.1 %copy-start.76 = (f32[288,2]{0,1:T(2,128)S(1)}, f32[288,2]{0,1:T(2,128)}, u32[]{:S(2)}) copy-start(f32[288,2]{0,1:T(2,128)} %param.51) | copy-start | bytes 6916
  798.9 51.1 %copy-start.77 = (f32[288,2]{0,1:T(2,128)S(1)}, f32[288,2]{0,1:T(2,128)}, u32[]{:S(2)}) copy-start(f32[288,2]{0,1:T(2,128)} %param.59) | copy-start | bytes 6916
  798.9 77.0 %copy-start.57 = (f32[288,12]{0,1:T(8,128)S(1)}, f32[288,12]{0,1:T(8,128)}, u32[]{:S(2)}) copy-start(f32[288,12]{0,1:T(8,128)} %param.38) | copy-start | bytes 41476
  798.9 77.0 %copy-start.70 = (f32[288,12]{0,1:T(8,128)S(1)}, f32[288,12]{0,1:T(8,128)}, u32[]{:S(2)}) copy-start(f32[288,12]{0,1:T(8,128)} %param.46) | copy-start | bytes 41476
  798.9 77.0 %copy-start.71 = (f32[288,12]{0,1:T(8,128)S(1)}, f32[288,12]{0,1:T(8,128)}, u32[]{:S(2)}) copy-start(f32[288,12]{0,1:T(8,128)} %param.54) | copy-start | bytes 41476
  802.1 80.8 %copy-start.58 = (f32[288,12]{0,1:T(8,128)S(1)}, f32[288,12]{0,1:T(8,128)}, u32[]{:S(2)}) copy-start(f32[288,12]{0,1:T(8,128)} %param.37) | copy-start | bytes 41476
  802.1 80.8 %copy-start.72 = (f32[288,12]{0,1:T(8,128)S(1)}, f32[288,12]{0,1:T(8,128)}, u32[]{:S(2)}) copy-start(f32[288,12]{0,1:T(8,128)} %param.45) | copy-start | bytes 41476
  802.1 80.8 %copy-start.73 = (f32[288,12]{0,1:T(8,128)S(1)}, f32[288,12]{0,1:T(8,128)}, u32[]{:S(2)}) copy-start(f32[288,12]{0,1:T(8,128)} %param.53) | copy-start | bytes 41476
  802.1 58.0 %collective-permute-start.6 = (bf16[576,16]{0,1:T(8,128)(2,1)S(1)}, bf16[576,16]{0,1:T(8,128)(2,1)S(1)}, u32[]{:S(2)}, u32[]{:S(2)}) collective-permute-start(bf16[576,16]{0,1:T(8,128)(2,1)S(1)} %get-tuple-element.424), channel_id=1, source_target_pairs={{0,6},{2,8},{4,10},{6,12},{8,14},{10,16},{12,18},{14,20},{16,22},{... | collective-permute-start | bytes 55304
  805.3 46.6 %collective-permute-start.10 = (bf16[576,16]{0,1:T(8,128)(2,1)S(1)}, bf16[576,16]{0,1:T(8,128)(2,1)S(1)}, u32[]{:S(2)}, u32[]{:S(2)}) collective-permute-start(bf16[576,16]{0,1:T(8,128)(2,1)S(1)} %get-tuple-element.425), channel_id=1, source_target_pairs={{0,6},{2,8},{4,10},{6,12},{8,14},{10,16},{12,18},{14,20},{16,22},{... | collective-permute-start | bytes 55304
  813.1 40.1 %collective-permute-start.9 = (bf16[576,16]{0,1:T(8,128)(2,1)S(1)}, bf16[576,16]{0,1:T(8,128)(2,1)S(1)}, u32[]{:S(2)}, u32[]{:S(2)}) collective-permute-start(bf16[576,16]{0,1:T(8,128)(2,1)S(1)} %get-tuple-element.425), channel_id=1, source_target_pairs={{0,4},{2,6},{4,8},{6,10},{8,12},{10,14},{12,16},{14,18},{16,20},{1... | collective-permute-start | bytes 55304
  814.4 40.1 %collective-permute-start.8 = (bf16[576,16]{0,1:T(8,128)(2,1)S(1)}, bf16[576,16]{0,1:T(8,128)(2,1)S(1)}, u32[]{:S(2)}, u32[]{:S(2)}) collective-permute-start(bf16[576,16]{0,1:T(8,128)(2,1)S(1)} %get-tuple-element.425), channel_id=1, source_target_pairs={{0,2},{2,4},{4,6},{6,8},{8,10},{10,12},{12,14},{14,16},{16,18},{18... | collective-permute-start | bytes 55304
  850.6 11.4 %collective-permute-start.5 = (bf16[576,16]{0,1:T(8,128)(2,1)S(1)}, bf16[576,16]{0,1:T(8,128)(2,1)S(1)}, u32[]{:S(2)}, u32[]{:S(2)}) collective-permute-start(bf16[576,16]{0,1:T(8,128)(2,1)S(1)} %get-tuple-element.424), channel_id=1, source_target_pairs={{0,4},{2,6},{4,8},{6,10},{8,12},{10,14},{12,16},{14,18},{16,20},{1... | collective-permute-start | bytes 55304
  851.9 18.3 %collective-permute-start.4 = (bf16[576,16]{0,1:T(8,128)(2,1)S(1)}, bf16[576,16]{0,1:T(8,128)(2,1)S(1)}, u32[]{:S(2)}, u32[]{:S(2)}) collective-permute-start(bf16[576,16]{0,1:T(8,128)(2,1)S(1)} %get-tuple-element.424), channel_id=1, source_target_pairs={{0,2},{2,4},{4,6},{6,8},{8,10},{10,12},{12,14},{14,16},{16,18},{18... | collective-permute-start | bytes 55304
  853.2 33.9 %collective-permute-start.2 = (bf16[576,48]{0,1:T(8,128)(2,1)S(1)}, bf16[576,48]{0,1:T(8,128)(2,1)S(1)}, u32[]{:S(2)}, u32[]{:S(2)}) collective-permute-start(bf16[576,48]{0,1:T(8,128)(2,1)S(1)} %get-tuple-element.423), channel_id=1, source_target_pairs={{0,6},{2,8},{4,10},{6,12},{8,14},{10,16},{12,18},{14,20},{16,22},{... | collective-permute-start | bytes 165896
  854.5 3.9 collective-permute-start.7
  858.3 23.6 %reduce-scatter.48.cloned.1.call-start = ((), (), s32[]{:S(2)}) async-start(), calls=%async_computation.20 | async-start | bytes 221184
  858.4 30.1 %collective-permute-start.1 = (bf16[576,48]{0,1:T(8,128)(2,1)S(1)}, bf16[576,48]{0,1:T(8,128)(2,1)S(1)}, u32[]{:S(2)}, u32[]{:S(2)}) collective-permute-start(bf16[576,48]{0,1:T(8,128)(2,1)S(1)} %get-tuple-element.423), channel_id=1, source_target_pairs={{0,4},{2,6},{4,8},{6,10},{8,12},{10,14},{12,16},{14,18},{16,20},{1... | collective-permute-start | bytes 165896
  860.1 32.4 %collective-permute-start = (bf16[576,48]{0,1:T(8,128)(2,1)S(1)}, bf16[576,48]{0,1:T(8,128)(2,1)S(1)}, u32[]{:S(2)}, u32[]{:S(2)}) collective-permute-start(bf16[576,48]{0,1:T(8,128)(2,1)S(1)} %get-tuple-element.423), channel_id=1, source_target_pairs={{0,2},{2,4},{4,6},{6,8},{8,10},{10,12},{12,14},{14,16},{16,18},{18... | collective-permute-start | bytes 165896
  862.0 39.3 %collective-permute-start.14 = (bf16[576,48]{0,1:T(8,128)(2,1)S(1)}, bf16[576,48]{0,1:T(8,128)(2,1)S(1)}, u32[]{:S(2)}, u32[]{:S(2)}) collective-permute-start(bf16[576,48]{0,1:T(8,128)(2,1)S(1)} %get-tuple-element.426), channel_id=1, source_target_pairs={{0,6},{2,8},{4,10},{6,12},{8,14},{10,16},{12,18},{14,20},{16,22},{... | collective-permute-start | bytes 165896
  870.2 13.4 %collective-permute-start.3 = (bf16[576,36]{0,1:T(8,128)(2,1)S(1)}, bf16[576,36]{0,1:T(8,128)(2,1)S(1)}, u32[]{:S(2)}, u32[]{:S(2)}) collective-permute-start(bf16[576,36]{0,1:T(8,128)(2,1)S(1)} %slice.82), channel_id=1, source_target_pairs={{0,8},{2,10},{4,12},{6,14},{8,16},{10,18},{12,20},{14,22},{16,24},... | collective-permute-start | bytes 124424
  874.8 31.8 %reduce-scatter.46.cloned.1.call-start = ((), (), s32[]{:S(2)}) async-start(), calls=%async_computation.19 | async-start | bytes 221184
  883.6 17.7 %collective-permute-start.13 = (bf16[576,48]{0,1:T(8,128)(2,1)S(1)}, bf16[576,48]{0,1:T(8,128)(2,1)S(1)}, u32[]{:S(2)}, u32[]{:S(2)}) collective-permute-start(bf16[576,48]{0,1:T(8,128)(2,1)S(1)} %get-tuple-element.426), channel_id=1, source_target_pairs={{0,4},{2,6},{4,8},{6,10},{8,12},{10,14},{12,16},{14,18},{16,20},{1... | collective-permute-start | bytes 165896
  887.1 14.2 %collective-permute-start.12 = (bf16[576,48]{0,1:T(8,128)(2,1)S(1)}, bf16[576,48]{0,1:T(8,128)(2,1)S(1)}, u32[]{:S(2)}, u32[]{:S(2)}) collective-permute-start(bf16[576,48]{0,1:T(8,128)(2,1)S(1)} %get-tuple-element.426), channel_id=1, source_target_pairs={{0,2},{2,4},{4,6},{6,8},{8,10},{10,12},{12,14},{14,16},{16,18},{18... | collective-permute-start | bytes 165896
  888.5 14.8 %collective-permute-start.16 = (bf16[1536,40]{0,1:T(8,128)(2,1)S(1)}, bf16[1536,40]{0,1:T(8,128)(2,1)S(1)}, u32[]{:S(2)}, u32[]{:S(2)}) collective-permute-start(bf16[1536,40]{0,1:T(8,128)(2,1)S(1)} %get-tuple-element.427), channel_id=1, source_target_pairs={{0,2},{2,4},{4,6},{6,8},{8,10},{10,12},{12,14},{14,16},{16,18},{18... | collective-permute-start | bytes 368648
  892.5 5.4 collective-permute-start.15
  897.9 21.4 %reduce-scatter.52.cloned.1.call-start = ((), (), s32[]{:S(2)}) async-start(), calls=%async_computation.22 | async-start | bytes 221184
  897.9 5.4 collective-permute-start.17
  903.2 29.0 %reduce-scatter.42.cloned.1.call-start = ((), (), s32[]{:S(2)}) async-start(), calls=%async_computation.16 | async-start | bytes 184320 | tf_op jit(solution)/shard_map/reduce_scatter | solution.py:168
  (84 other events, 673.3 us)
Sparse Core Ops, SparseCore 0:
  14.3 43.5 all-gather.20
  76.4 93.4 all-gather.14
  172.8 39.4 all-gather.18
  215.0 39.7 all-gather.16
  322.4 59.8 reduce-scatter.37
  385.9 60.1 reduce-scatter.39
  448.9 9.4 reduce-scatter.53
  460.6 10.4 reduce-scatter.55
  618.3 110.3 reduce-scatter.43
  798.9 13.6 reduce-scatter.57
  858.5 10.5 reduce-scatter.49
  875.0 6.9 reduce-scatter.47
  898.0 8.5 reduce-scatter.45
  908.8 10.4 reduce-scatter.51
  922.0 10.1 reduce-scatter.41
where the time goes:
time: 948 us; the launch traced here: 941 us
  waiting for transfers between devices  220 us (23%)
  matrix products  220 us (23%)
  blocking collectives  212 us (22%)
  local copies, waits for them, and re-layouts  129 us (14%)
  other arithmetic  78.6 us (8%)
  starting transfers between devices  54.4 us (6%)
  between operations  17 us (2%)
    unnamed x41, waiting for transfers between devices  92.8 us
    unnamed x218, local copies, waits for them, and re-layouts  78.4 us
    reduce_scatter x1, waiting for transfers between devices, sum_columns(): lax.psum_scatter(up_part.astype(jnp.bfloat16), 'ctx', scatter_dimension=1...  59.6 us
    unnamed x26, starting transfers between devices  53.7 us
    unnamed x1, blocking collectives  52.1 us
    dot_general x8, matrix products, masked_scores(): jnp.einsum('srjgd,stjd->sjgrt', query_five, keys_four, preferred_element_...  49.8 us
    reduce_scatter x1, waiting for transfers between devices, sum_columns(): lax.psum_scatter(gate_part.astype(jnp.bfloat16), 'ctx', scatter_dimension...  42.6 us
    reduce_sum x4, other arithmetic, stats_step(): jnp.sum(jnp.exp(scores - new_top[..., None]), axis=-1)  35.7 us
  transfers between devices with their start and end apart: 33, of which 8 were waited for; matrix products, arithmetic and copies ran while one was open for 42% of the time, Pallas kernels for 0%

commit v1 on v0

v1 whole, which is shorter than its diff:
```python
import functools

import jax
import jax.numpy as jnp
from jax import lax
from jax.experimental import pallas as pl
from jax.experimental.pallas import tpu as pltpu
from jax.sharding import PartitionSpec as P

MODEL_WIDTH = 576
FF = 1536
HEADS = 9
KV_HEADS = 3
HEAD_DIM = 64
STEP = 10
GROUP = HEADS // KV_HEADS
KEY_WIDTH = KV_HEADS * HEAD_DIM
QUERY_WIDTH = HEADS * HEAD_DIM
PACK = 2 * HEAD_DIM
KV_PACKED = KV_HEADS * PACK
TILE = 256
FF_CHUNK = 512

NORM_EPS = 1e-05
ROPE_BASE = 100000.0
BETA_ONE = 0.9
BETA_TWO = 0.95
ADAM_EPS = 1e-08
DECAY = 0.1
GAIN_RATE = 0.5
MASKED = -1e30
VMEM_BYTES = 56 * 1024 * 1024

f32 = jnp.float32
bf16 = jnp.bfloat16


def dot_nt(a, b):
    return lax.dot_general(a, b, (((1,), (1,)), ((), ())), preferred_element_type=f32)


def dot_nn(a, b):
    return lax.dot_general(a, b, (((1,), (0,)), ((), ())), preferred_element_type=f32)


def lanes_of(shape):
    return lax.broadcasted_iota(jnp.int32, shape, len(shape) - 1)


def turned(v, first):
    lane = lanes_of(v.shape) % HEAD_DIM
    ahead = pltpu.roll(v, PACK - HEAD_DIM // 2, 1)
    behind = pltpu.roll(v, HEAD_DIM // 2, 1)
    if first:
        return jnp.where(lane < HEAD_DIM // 2, -ahead, behind)
    return jnp.where(lane < HEAD_DIM // 2, ahead, -behind)


def project_kernel(x_ref, gain_ref, weight_ref, cos_ref, sin_ref, normed_ref, query_ref, kv_ref):
    rows = x_ref.shape[1]
    blk = query_ref.shape[3] // GROUP
    x = x_ref[0].astype(f32)
    inv = lax.rsqrt(jnp.mean(x * x, axis=-1, keepdims=True) + NORM_EPS)
    normed = (x * inv * gain_ref[...]).astype(bf16)
    normed_ref[0] = normed
    raw = dot_nt(normed, weight_ref[...])
    cosine, sine = cos_ref[0], sin_ref[0]
    low_half = lanes_of((rows, PACK)) < HEAD_DIM
    for j in range(KV_HEADS):
        part = raw[:, j * PACK : (j + 1) * PACK]
        spun = part * cosine + turned(part, True) * sine
        kv_ref[0, :, j * PACK : (j + 1) * PACK] = jnp.where(low_half, spun, part).astype(bf16)
    for i in range((HEADS + 1) // 2):
        begin = KV_PACKED + i * PACK
        if 2 * i + 1 < HEADS:
            part = raw[:, begin : begin + PACK]
        else:
            tail = raw[:, begin : begin + HEAD_DIM]
            part = jnp.concatenate([tail, tail], axis=1)
        spun = part * cosine + turned(part, True) * sine
        spun = spun.astype(bf16).astype(f32) * (HEAD_DIM**-0.5)
        pair = [jnp.where(low_half, spun, 0.0)]
        if 2 * i + 1 < HEADS:
            pair.append(jnp.where(low_half, pltpu.roll(spun, HEAD_DIM, 1), 0.0))
        for offset, value in enumerate(pair):
            head = 2 * i + offset
            j, member = head // GROUP, head % GROUP
            value = value.astype(bf16)
            for b in range(rows // blk):
                query_ref[0, b, j, member * blk : (member + 1) * blk, :] = value[
                    b * blk : (b + 1) * blk
                ]


def sort_blocks(blocks_ref, s, kv_ref, sorted_ref, blk):
    chunks, _, rows, _ = kv_ref.shape
    per = rows // blk
    for g in range(chunks):
        for b in range(per):
            place = pl.multiple_of(blocks_ref[s, g * per + b] * blk, blk)
            sorted_ref[pl.ds(place, blk), :] = kv_ref[g, 0, b * blk : (b + 1) * blk, :]


def allowed_mask(place, tile_begin, blk, rows):
    row = lax.broadcasted_iota(jnp.int32, (rows, TILE), 0) % blk
    col = lax.broadcasted_iota(jnp.int32, (rows, TILE), 1)
    return col <= row + (place * blk - tile_begin)


def attend_kernel(
    blocks_ref, own_ref, query_ref, kv_ref, out_ref, log_ref, sorted_ref, score_ref, top_ref, acc_ref
):
    s = pl.program_id(0)
    per, rows = query_ref.shape[1], query_ref.shape[3]
    blk = rows // GROUP
    sort_blocks(blocks_ref, s, kv_ref, sorted_ref, blk)
    lane = lanes_of((TILE, PACK))
    for b in range(per):
        place = own_ref[s, b]
        full = (place * blk) // TILE

        def score_tile(t, masked):
            begin = pl.multiple_of(t * TILE, TILE)
            for j in range(KV_HEADS):
                kv = sorted_ref[pl.ds(begin, TILE), j * PACK : (j + 1) * PACK]
                score = dot_nt(query_ref[0, b, j], kv)
                if masked:
                    score = jnp.where(allowed_mask(place, begin, blk, rows), score, MASKED)
                score_ref[j, t] = score
                best = jnp.maximum(score[:, :PACK], score[:, PACK:])
                top_ref[j] = jnp.maximum(top_ref[j], best)

        top_ref[...] = jnp.full(top_ref.shape, MASKED, f32)
        acc_ref[...] = jnp.zeros(acc_ref.shape, f32)

        @pl.loop(0, full)
        def _(t):
            score_tile(t, False)

        score_tile(full, True)
        for j in range(KV_HEADS):
            top = jnp.max(top_ref[j], axis=-1, keepdims=True)
            top_ref[j] = jnp.broadcast_to(top, (rows, PACK))

        @pl.loop(0, full + 1)
        def _(t):
            begin = pl.multiple_of(t * TILE, TILE)
            for j in range(KV_HEADS):
                kv = sorted_ref[pl.ds(begin, TILE), j * PACK : (j + 1) * PACK]
                ones_v = jnp.where(lane < HEAD_DIM, jnp.ones((), bf16), kv)
                top = top_ref[j]
                score = score_ref[j, t]
                prob = jnp.concatenate(
                    [jnp.exp(score[:, :PACK] - top), jnp.exp(score[:, PACK:] - top)], axis=1
                )
                acc_ref[j] += dot_nn(prob.astype(bf16), ones_v)

        for j in range(KV_HEADS):
            acc = acc_ref[j]
            low_half = lanes_of(acc.shape) < HEAD_DIM
            total = jnp.where(low_half, acc, pltpu.roll(acc, HEAD_DIM, 1))
            log_ref[0, b, j] = top_ref[j] + jnp.log(total)
            attended = (acc / total).astype(bf16)
            for member in range(GROUP):
                head = j * GROUP + member
                out_ref[0, b * blk : (b + 1) * blk, head * HEAD_DIM : (head + 1) * HEAD_DIM] = (
                    attended[member * blk : (member + 1) * blk, HEAD_DIM:]
                )


def middle_kernel(
    x_ref,
    attn_ref,
    cot_ref,
    gain_ref,
    out_w_ref,
    gate_w_ref,
    up_w_ref,
    down_w_ref,
    block_ref,
    normed_ref,
    hidden_ref,
    dgate_ref,
    dup_ref,
    dattn_ref,
    dout_ref,
    dresid_ref,
    gain_grad_ref,
):
    attn = attn_ref[0]
    cot = cot_ref[0]
    resid = x_ref[0].astype(f32) + dot_nt(attn, out_w_ref[...])
    inv = lax.rsqrt(jnp.mean(resid * resid, axis=-1, keepdims=True) + NORM_EPS)
    hat = resid * inv
    gain = gain_ref[...]
    normed = (hat * gain).astype(bf16)
    normed_ref[0] = normed
    block = resid
    dnormed = jnp.zeros(resid.shape, f32)
    for begin in range(0, FF, FF_CHUNK):
        span = slice(begin, begin + FF_CHUNK)
        gate = dot_nt(normed, gate_w_ref[span, :])
        up = dot_nt(normed, up_w_ref[span, :])
        sig = 1.0 / (1.0 + jnp.exp(-gate))
        act = gate * sig
        hidden = (act * up).astype(bf16)
        hidden_ref[0, :, span] = hidden
        block = block + dot_nt(hidden, down_w_ref[:, span])
        dhidden = dot_nn(cot, down_w_ref[:, span])
        dgate = (dhidden * up * (sig * (1.0 + gate * (1.0 - sig)))).astype(bf16)
        dup = (dhidden * act).astype(bf16)
        dgate_ref[0, :, span] = dgate
        dup_ref[0, :, span] = dup
        dnormed = dnormed + dot_nn(dgate, gate_w_ref[span, :]) + dot_nn(dup, up_w_ref[span, :])
    block_ref[0] = block
    gain_grad_ref[0] = jnp.sum(dnormed * hat, axis=0, keepdims=True)
    scaled = dnormed * gain
    dresid = cot.astype(f32) + inv * (scaled - hat * jnp.mean(scaled * hat, axis=-1, keepdims=True))
    dresid_ref[0] = dresid
    dattn = dresid.astype(bf16)
    dattn_ref[0] = dattn
    dout_ref[0] = dot_nn(dattn, out_w_ref[...]).astype(bf16)


def attend_back_kernel(
    blocks_ref,
    own_ref,
    query_ref,
    kv_ref,
    out_ref,
    dout_ref,
    log_ref,
    cos_ref,
    sin_ref,
    dquery_ref,
    dkv_ref,
    sorted_ref,
    both_ref,
    flip_ref,
    delta_ref,
    dq_ref,
    dkv_t_ref,
    dkv_s_ref,
):
    s = pl.program_id(0)
    per, rows = query_ref.shape[1], query_ref.shape[3]
    blk = rows // GROUP
    length = sorted_ref.shape[0]
    sort_blocks(blocks_ref, s, kv_ref, sorted_ref, blk)
    dkv_t_ref[...] = jnp.zeros(dkv_t_ref.shape, f32)
    for b in range(per):
        place = own_ref[s, b]
        full = (place * blk) // TILE
        span = slice(b * blk, (b + 1) * blk)
        for j in range(KV_HEADS):
            both_ref[j, :rows] = query_ref[0, b, j]
            for member in range(GROUP):
                head = j * GROUP + member
                lanes = slice(head * HEAD_DIM, (head + 1) * HEAD_DIM)
                dout = dout_ref[0, span, lanes]
                delta = jnp.sum(
                    dout.astype(f32) * out_ref[0, span, lanes].astype(f32), axis=-1, keepdims=True
                )
                here = slice(member * blk, (member + 1) * blk)
                delta_ref[j, here] = jnp.broadcast_to(delta, (blk, PACK))
                both_ref[j, rows + member * blk : rows + (member + 1) * blk] = jnp.concatenate(
                    [jnp.zeros_like(dout), dout], axis=1
                )
            flip_ref[j] = both_ref[j].T
        dq_ref[...] = jnp.zeros(dq_ref.shape, f32)

        def tile_step(t, masked):
            begin = pl.multiple_of(t * TILE, TILE)
            for j in range(KV_HEADS):
                kv = sorted_ref[pl.ds(begin, TILE), j * PACK : (j + 1) * PACK]
                score = dot_nt(both_ref[j, :rows], kv)
                dprob = dot_nt(both_ref[j, rows:], kv)
                log_total = log_ref[0, b, j]
                delta = delta_ref[j]
                prob = jnp.concatenate(
                    [jnp.exp(score[:, :PACK] - log_total), jnp.exp(score[:, PACK:] - log_total)],
                    axis=1,
                )
                if masked:
                    prob = jnp.where(allowed_mask(place, begin, blk, rows), prob, 0.0)
                dscore = prob * jnp.concatenate(
                    [dprob[:, :PACK] - delta, dprob[:, PACK:] - delta], axis=1
                )
                dscore = dscore.astype(bf16)
                dq_ref[j] += dot_nn(dscore, kv)
                joint = jnp.concatenate([dscore, prob.astype(bf16)], axis=0)
                dkv_t_ref[j * PACK : (j + 1) * PACK, pl.ds(begin, TILE)] += dot_nn(
                    flip_ref[j], joint
                )

        @pl.loop(0, full)
        def _(t):
            tile_step(t, False)

        tile_step(full, True)
        cosine, sine = cos_ref[0, span, :], sin_ref[0, span, :]
        for j in range(KV_HEADS):
            for member in range(GROUP):
                head = j * GROUP + member
                grad = dq_ref[j, member * blk : (member + 1) * blk]
                back = (grad * cosine + turned(grad, False) * sine) * (HEAD_DIM**-0.5)
                dquery_ref[0, span, head * HEAD_DIM : (head + 1) * HEAD_DIM] = back[
                    :, :HEAD_DIM
                ].astype(bf16)
    for begin in range(0, length, TILE):
        dkv_s_ref[begin : begin + TILE, :] = dkv_t_ref[:, begin : begin + TILE].T.astype(bf16)
    for g in range(kv_ref.shape[0]):
        for b in range(per):
            place = pl.multiple_of(blocks_ref[s, g * per + b] * blk, blk)
            dkv_ref[g, 0, b * blk : (b + 1) * blk, :] = dkv_s_ref[pl.ds(place, blk), :]


def final_kernel(
    x_ref,
    gain_ref,
    dquery_ref,
    dkv_ref,
    dresid_ref,
    cos_ref,
    sin_ref,
    weight_ref,
    dinput_ref,
    dall_ref,
    gain_grad_ref,
):
    rows = x_ref.shape[1]
    cosine, sine = cos_ref[0], sin_ref[0]
    low_half = lanes_of((rows, PACK)) < HEAD_DIM
    for j in range(KV_HEADS):
        part = dkv_ref[0, :, j * PACK : (j + 1) * PACK].astype(f32)
        back = part * cosine + turned(part, False) * sine
        dall_ref[0, :, j * PACK : (j + 1) * PACK] = jnp.where(low_half, back, part).astype(bf16)
    dall_ref[0, :, KV_PACKED:] = dquery_ref[0]
    dnormed = dot_nn(dall_ref[0], weight_ref[...])
    x = x_ref[0].astype(f32)
    inv = lax.rsqrt(jnp.mean(x * x, axis=-1, keepdims=True) + NORM_EPS)
    hat = x * inv
    gain_grad_ref[0] = jnp.sum(dnormed * hat, axis=0, keepdims=True)
    scaled = dnormed * gain_ref[...]
    dinput_ref[0] = dresid_ref[0] + inv * (
        scaled - hat * jnp.mean(scaled * hat, axis=-1, keepdims=True)
    )


def one(shape):
    rest = tuple(shape[1:])
    return pl.BlockSpec((1,) + rest, lambda s, *_: (s,) + (0,) * len(rest))


def whole(shape):
    return pl.BlockSpec(tuple(shape), lambda s, *_: (0,) * len(shape))


def second(shape):
    rest = tuple(shape[2:])
    return pl.BlockSpec((shape[0], 1) + rest, lambda s, *_: (0, s) + (0,) * len(rest))


def call(kernel, seqs, inputs, outputs, scalars=(), scratch=(), flops=0):
    in_specs = [make(array.shape) for make, array in inputs]
    out_specs = [make(shape) for make, shape, _ in outputs]
    moved = sum(array.size * array.dtype.itemsize for _, array in inputs)
    for _, shape, kind in outputs:
        count = 1
        for size in shape:
            count *= size
        moved += count * jnp.dtype(kind).itemsize
    return pl.pallas_call(
        kernel,
        grid_spec=pltpu.PrefetchScalarGridSpec(
            num_scalar_prefetch=len(scalars),
            grid=(seqs,),
            in_specs=in_specs,
            out_specs=out_specs,
            scratch_shapes=list(scratch),
        ),
        out_shape=[jax.ShapeDtypeStruct(shape, kind) for _, shape, kind in outputs],
        compiler_params=pltpu.CompilerParams(vmem_limit_bytes=VMEM_BYTES),
        cost_estimate=pl.CostEstimate(
            flops=int(flops), bytes_accessed=int(moved), transcendentals=0
        ),
    )(*scalars, *[array for _, array in inputs])


def adam_update(weight, first, second, grad, rate, decay):
    first_next = BETA_ONE * first + (1.0 - BETA_ONE) * grad
    second_next = BETA_TWO * second + (1.0 - BETA_TWO) * grad * grad
    first_fix = first_next / (1.0 - BETA_ONE**STEP)
    second_fix = second_next / (1.0 - BETA_TWO**STEP)
    update = first_fix / (jnp.sqrt(second_fix) + ADAM_EPS) + decay * weight
    return (weight - rate * update, first_next, second_next)


def gather_packed(packed):
    ctx, fsdp = lax.axis_size("ctx"), lax.axis_size("fsdp")
    rows, lanes = packed.shape
    every = lax.all_gather(packed, ("ctx", "fsdp"), axis=0, tiled=False)
    every = every.reshape(ctx, fsdp, rows, lanes).transpose(0, 2, 1, 3)
    return every.reshape(ctx, rows, fsdp * lanes)


def scatter_packed(grads):
    ctx, fsdp = lax.axis_size("ctx"), lax.axis_size("fsdp")
    rows, lanes = grads.shape[1], grads.shape[2] // fsdp
    split = grads.astype(bf16).reshape(ctx, rows, fsdp, lanes).transpose(0, 2, 1, 3)
    split = split.reshape(ctx * fsdp, rows, lanes)
    return lax.psum_scatter(split, ("ctx", "fsdp"), scatter_dimension=0, tiled=False).astype(f32)


def weight_grad(left, right):
    return lax.dot_general(left, right, (((0, 1), (0, 1)), ((), ())), preferred_element_type=f32)


def body(
    tokens,
    cotangent,
    pair_order,
    query_weight,
    key_master_weight,
    value_master_weight,
    output_weight,
    gate_weight,
    up_weight,
    down_weight,
    norm_gains,
    query_first,
    key_first_moment,
    value_first_moment,
    output_first,
    gate_first,
    up_first,
    down_first,
    gains_first,
    query_second,
    key_second_moment,
    value_second_moment,
    output_second,
    gate_second,
    up_second,
    down_second,
    gains_second,
):
    masters = (
        query_weight,
        key_master_weight,
        value_master_weight,
        output_weight,
        gate_weight,
        up_weight,
        down_weight,
    )
    ctx = lax.axis_size("ctx")
    index = lax.axis_index("ctx")
    chunks = ctx // 2
    core = index % 2
    seqs = tokens.shape[0] // 2
    part_rows = tokens.shape[1]
    rows = 2 * part_rows
    blk = part_rows // 2
    per = rows // blk
    length = part_rows * ctx
    mine, other = core * seqs, (1 - core) * seqs
    partners = [(i, i ^ 1) for i in range(ctx)]
    cores = [list(range(0, ctx, 2)), list(range(1, ctx, 2))]

    def take(array):
        own = lax.dynamic_slice_in_dim(array, mine, seqs, 0)
        got = lax.ppermute(lax.dynamic_slice_in_dim(array, other, seqs, 0), "ctx", partners)
        return jnp.concatenate([own, got], axis=1)

    def give(array):
        got = lax.ppermute(array[:, part_rows:], "ctx", partners)
        result = jnp.zeros((2 * seqs, part_rows) + array.shape[2:], array.dtype)
        result = lax.dynamic_update_slice_in_dim(result, array[:, :part_rows], mine, 0)
        return lax.dynamic_update_slice_in_dim(result, got, other, 0)

    turned_low = [matrix.astype(bf16).T for matrix in masters]
    gains_low = norm_gains.astype(bf16).T
    first_pack = gather_packed(jnp.concatenate(turned_low[:3] + [gains_low], axis=0))
    second_pack = gather_packed(jnp.concatenate(turned_low[3:6], axis=0))
    down_t = gather_packed(turned_low[6]).reshape(MODEL_WIDTH, FF)
    q_cols, kv_cols = QUERY_WIDTH // ctx, KEY_WIDTH // ctx
    query_t = first_pack[:, :q_cols].reshape(QUERY_WIDTH, MODEL_WIDTH)
    key_t = first_pack[:, q_cols : q_cols + kv_cols].reshape(KV_HEADS, HEAD_DIM, MODEL_WIDTH)
    value_t = first_pack[:, q_cols + kv_cols : q_cols + 2 * kv_cols].reshape(
        KV_HEADS, HEAD_DIM, MODEL_WIDTH
    )
    gains = first_pack[0, q_cols + 2 * kv_cols :].astype(f32)
    gain_one, gain_two = gains[0:1], gains[1:2]
    inward = jnp.concatenate(
        [jnp.stack([key_t, value_t], axis=1).reshape(KV_PACKED, MODEL_WIDTH), query_t], axis=0
    )
    o_cols, f_cols = MODEL_WIDTH // ctx, FF // ctx
    output_t = second_pack[:, :o_cols].reshape(MODEL_WIDTH, QUERY_WIDTH)
    gate_t = second_pack[:, o_cols : o_cols + f_cols].reshape(FF, MODEL_WIDTH)
    up_t = second_pack[:, o_cols + f_cols :].reshape(FF, MODEL_WIDTH)

    x = take(tokens)
    cot = take(cotangent)
    order = lax.dynamic_slice_in_dim(pair_order, mine, seqs, 0)
    ends = jnp.stack([order, 2 * ctx - 1 - order], axis=2).reshape(seqs, chunks, 2, 2)
    ends = jnp.where(core == 0, ends, ends[:, :, ::-1])
    own = lax.dynamic_slice_in_dim(ends, index // 2, 1, 1).reshape(seqs, per)
    blocks = ends.reshape(seqs, chunks * per)
    places = (own[:, :, None] * blk + jnp.arange(blk, dtype=jnp.int32)).reshape(seqs, rows)
    half_dim = HEAD_DIM // 2
    inverse = ROPE_BASE ** (-jnp.arange(half_dim, dtype=f32) * 2.0 / HEAD_DIM)
    angle = places.astype(f32)[..., None] * inverse
    cosine = jnp.tile(jnp.cos(angle), (1, 1, PACK // half_dim))
    sine = jnp.tile(jnp.sin(angle), (1, 1, PACK // half_dim))

    wide = (seqs, rows, MODEL_WIDTH)
    heads = (seqs, per, KV_HEADS, GROUP * blk, PACK)
    normed_one, query, kv = call(
        project_kernel,
        seqs,
        [(one, x), (whole, gain_one), (whole, inward), (one, cosine), (one, sine)],
        [(one, wide, bf16), (one, heads, bf16), (one, (seqs, rows, KV_PACKED), bf16)],
        flops=2 * seqs * rows * MODEL_WIDTH * (KV_PACKED + QUERY_WIDTH),
    )
    kv_all = lax.all_gather(kv, "ctx", axis=0, tiled=False, axis_index_groups=cores)
    pairs = seqs * HEADS * rows * length * HEAD_DIM
    tile_rows = (KV_HEADS, GROUP * blk, PACK)
    attn, logs = call(
        attend_kernel,
        seqs,
        [(one, query), (second, kv_all)],
        [(one, wide, bf16), (one, heads, f32)],
        scalars=(blocks, own),
        scratch=[
            pltpu.VMEM((length, KV_PACKED), bf16),
            pltpu.VMEM((KV_HEADS, length // TILE, GROUP * blk, TILE), f32),
            pltpu.VMEM(tile_rows, f32),
            pltpu.VMEM(tile_rows, f32),
        ],
        flops=4 * pairs,
    )
    ff_wide = (seqs, rows, FF)
    (
        block_local,
        normed_two,
        hidden,
        dgate,
        dup,
        dattn,
        dout,
        dresid,
        gain_two_grad,
    ) = call(
        middle_kernel,
        seqs,
        [
            (one, x),
            (one, attn),
            (one, cot),
            (whole, gain_two),
            (whole, output_t),
            (whole, gate_t),
            (whole, up_t),
            (whole, down_t),
        ],
        [
            (one, wide, f32),
            (one, wide, bf16),
            (one, ff_wide, bf16),
            (one, ff_wide, bf16),
            (one, ff_wide, bf16),
            (one, wide, bf16),
            (one, wide, bf16),
            (one, wide, f32),
            (one, (seqs, 1, MODEL_WIDTH), f32),
        ],
        flops=2 * seqs * rows * MODEL_WIDTH * (6 * FF + 2 * MODEL_WIDTH),
    )
    block_output = give(block_local)
    down_grad = weight_grad(cot, hidden).reshape(ctx, o_cols, FF)
    gate_grad = weight_grad(dgate, normed_two).reshape(ctx, f_cols, MODEL_WIDTH)
    up_grad = weight_grad(dup, normed_two).reshape(ctx, f_cols, MODEL_WIDTH)
    output_grad = weight_grad(dattn, attn).reshape(ctx, o_cols, QUERY_WIDTH)
    down_sum = scatter_packed(down_grad)
    second_sum = scatter_packed(jnp.concatenate([output_grad, gate_grad, up_grad], axis=1))

    dquery, dkv = call(
        attend_back_kernel,
        seqs,
        [
            (one, query),
            (second, kv_all),
            (one, attn),
            (one, dout),
            (one, logs),
            (one, cosine),
            (one, sine),
        ],
        [(one, wide, bf16), (second, kv_all.shape, bf16)],
        scalars=(blocks, own),
        scratch=[
            pltpu.VMEM((length, KV_PACKED), bf16),
            pltpu.VMEM((KV_HEADS, 2 * GROUP * blk, PACK), bf16),
            pltpu.VMEM((KV_HEADS, PACK, 2 * GROUP * blk), bf16),
            pltpu.VMEM(tile_rows, f32),
            pltpu.VMEM(tile_rows, f32),
            pltpu.VMEM((KV_PACKED, length), f32),
            pltpu.VMEM((length, KV_PACKED), bf16),
        ],
        flops=10 * pairs,
    )
    dkv_own = lax.psum_scatter(
        dkv, "ctx", scatter_dimension=0, tiled=False, axis_index_groups=cores
    )
    inner = KV_PACKED + QUERY_WIDTH
    dinput, dall, gain_one_grad = call(
        final_kernel,
        seqs,
        [
            (one, x),
            (whole, gain_one),
            (one, dquery),
            (one, dkv_own),
            (one, dresid),
            (one, cosine),
            (one, sine),
            (whole, inward),
        ],
        [
            (one, wide, f32),
            (one, (seqs, rows, inner), bf16),
            (one, (seqs, 1, MODEL_WIDTH), f32),
        ],
        flops=2 * seqs * rows * MODEL_WIDTH * inner,
    )
    input_gradient = give(dinput)
    inward_grad = weight_grad(dall, normed_one)
    kv_grad = inward_grad[:KV_PACKED].reshape(KV_HEADS, 2, HEAD_DIM, MODEL_WIDTH)
    key_grad = kv_grad[:, 0].reshape(ctx, kv_cols, MODEL_WIDTH)
    value_grad = kv_grad[:, 1].reshape(ctx, kv_cols, MODEL_WIDTH)
    query_grad = inward_grad[KV_PACKED:].reshape(ctx, q_cols, MODEL_WIDTH)
    gains_grad = jnp.concatenate(
        [jnp.sum(gain_one_grad, axis=0), jnp.sum(gain_two_grad, axis=0)], axis=0
    )
    gains_grad = jnp.broadcast_to(gains_grad[None], (ctx, 2, MODEL_WIDTH))
    first_sum = scatter_packed(
        jnp.concatenate([query_grad, key_grad, value_grad, gains_grad], axis=1)
    )
    reduced = (
        first_sum[:q_cols],
        first_sum[q_cols : q_cols + kv_cols],
        first_sum[q_cols + kv_cols : q_cols + 2 * kv_cols],
        second_sum[:o_cols],
        second_sum[o_cols : o_cols + f_cols],
        second_sum[o_cols + f_cols :],
        down_sum,
    )
    gains_total = first_sum[q_cols + 2 * kv_cols :].T
    rates = (
        (MODEL_WIDTH // 4) ** (-0.5),
        MODEL_WIDTH ** (-0.5),
        MODEL_WIDTH ** (-0.5),
        (MODEL_WIDTH // 32) ** (-0.5),
        MODEL_WIDTH ** (-0.5),
        MODEL_WIDTH ** (-0.5),
        (FF // 2) ** (-0.5),
    )
    firsts = (
        query_first,
        key_first_moment,
        value_first_moment,
        output_first,
        gate_first,
        up_first,
        down_first,
    )
    seconds = (
        query_second,
        key_second_moment,
        value_second_moment,
        output_second,
        gate_second,
        up_second,
        down_second,
    )
    results = [
        adam_update(
            masters[member], firsts[member], seconds[member], reduced[member].T, rates[member], DECAY
        )
        for member in range(7)
    ]
    results.append(adam_update(norm_gains, gains_first, gains_second, gains_total, GAIN_RATE, 0.0))
    new_weights = [result[0] for result in results]
    new_firsts = [result[1] for result in results]
    new_seconds = [result[2] for result in results]
    return tuple([block_output, input_gradient] + new_weights + new_firsts + new_seconds)


def solution(mesh):
    sequences = P("fsdp", "ctx", None)
    matrix = P("fsdp", "ctx")
    gains = P("fsdp", None)
    state = (matrix,) * 7 + (gains,)
    return jax.shard_map(
        body,
        mesh=mesh,
        in_specs=(sequences, sequences, P("fsdp", None)) + state * 3,
        out_specs=(sequences, sequences) + state * 3,
        check_vma=False,
    )
```

time: 948 us -> 819 us (0.86)
  waiting for transfers between devices: 220 us -> 526 us
  blocking collectives: 212 us -> 0 us
  matrix products: 220 us -> 16.7 us
  Pallas kernels: 0 us -> 127 us
  starting transfers between devices: 54.4 us -> 1.25 us
  other arithmetic: 78.6 us -> 26.8 us
  local copies, waits for them, and re-layouts: 129 us -> 95.7 us
    dot_general x49 -> x5, matrix products: 220 us -> 16.7 us  [weight_grad(): lax.dot_general(left, right, (((0, 1), (0, 1)), ((), ())), preferred_elem...]
    reduce_scatter x3 -> x4, waiting for transfers between devices: 113 us -> 315 us  [the longest x3 280 us: scatter_packed(): lax.psum_scatter(split, ('ctx', 'fsdp'), scatter_dimension=0, tiled=False)]
    all_gather x4, waiting for transfers between devices: 14 us -> 211 us  [the longest x3 150 us: gather_packed(): every = lax.all_gather(packed, ('ctx', 'fsdp'), axis=0, tiled=False)]
    all_gather x12 -> x0, blocking collectives: 129 us -> none  [the longest x1 24.6 us: gather_columns(): lax.all_gather(query_part, 'ctx', axis=1, tiled=True)]
    pallas_call x0 -> x5, Pallas kernels: none -> 127 us  [call(): pl.pallas_call(kernel, grid_spec=pltpu.PrefetchScalarGridSpec(num_scalar_...]
    unnamed x41 -> x8, waiting for transfers between devices: 92.8 us -> 0.13 us
    unnamed x218 -> x97, local copies, waits for them, and re-layouts: 78.4 us -> 18.5 us
    unnamed x26 -> x0, starting transfers between devices: 53.7 us -> none
  transfers between devices with their start and end apart: 33 -> 12, of which waited for: 8 -> 8; matrix products, arithmetic and copies ran while one was open for 42% -> 16% of each run, Pallas kernels for 0% -> 2%
where the time goes in v1:
time: 819 us; the launch traced here: 809 us
  waiting for transfers between devices  526 us (64%)
  Pallas kernels  127 us (16%)
  local copies, waits for them, and re-layouts  95.7 us (12%)
  other arithmetic  26.8 us (3%)
  matrix products  16.7 us (2%)
  between operations  15.2 us (2%)
    reduce_scatter x3, waiting for transfers between devices, scatter_packed(): lax.psum_scatter(split, ('ctx', 'fsdp'), scatter_dimension=0, tiled=False)  280 us
    all_gather x3, waiting for transfers between devices, gather_packed(): every = lax.all_gather(packed, ('ctx', 'fsdp'), axis=0, tiled=False)  150 us
    pallas_call x5, Pallas kernels, call(): pl.pallas_call(kernel, grid_spec=pltpu.PrefetchScalarGridSpec(num_scalar_...  127 us
    all_gather x1, waiting for transfers between devices, body(): lax.all_gather(kv, 'ctx', axis=0, tiled=False, axis_index_groups=cores)  61.5 us
    reduce_scatter x1, waiting for transfers between devices, body(): lax.psum_scatter(dkv, 'ctx', scatter_dimension=0, tiled=False, axis_index...  34.9 us
    reshape x4, local copies, waits for them, and re-layouts, scatter_packed(): split = split.reshape(ctx * fsdp, rows, lanes)  18.9 us
    unnamed x97, local copies, waits for them, and re-layouts  18.5 us
    dot_general x5, matrix products, weight_grad(): lax.dot_general(left, right, (((0, 1), (0, 1)), ((), ())), preferred_elem...  16.7 us
  transfers between devices with their start and end apart: 12, of which 8 were waited for; matrix products, arithmetic and copies ran while one was open for 16% of the time, Pallas kernels for 2%

profile of v1, /device:TPU:0, one launch (start us, length us, event | category | flops | bytes accessed | tf_op | source)
XLA Modules:
  0.0 809.3 jit_solution(3908854868549044370)
XLA Ops:
  10.4 1.5 convert_bitcast_fusion.3
  21.4 48.0 %all-gather.14.cloned.1.call-done = bf16[32,62,288]{2,1,0:T(8,128)(2,1)} async-done(((bf16[1,62,288]{2,1,0:T(8,128)(2,1)}), bf16[32,62,288]{2,1,0:T(8,128)(2,1)}) %all-gather.14.cloned.1.call-update) | async-done | bytes 1142800 | tf_op jit(solution)/shard_map/all_gather | solution.py:402
  69.3 3.0 copy.285
  78.0 6.3 shard_map.458
  87.9 40.1 %all-gather.18.cloned.1.call-done = bf16[32,36,768]{2,1,0:T(8,128)(2,1)} async-done(((bf16[1,36,768]{2,1,0:T(8,128)(2,1)}), bf16[32,36,768]{2,1,0:T(8,128)(2,1)}) %all-gather.18.cloned.1.call-update) | async-done | bytes 1769488 | tf_op jit(solution)/shard_map/all_gather | solution.py:402
  128.0 2.9 copy.232
  130.9 1.5 copy.283
  132.4 61.6 %all-gather.16.cloned.1.call-done = bf16[32,228,288]{1,2,0:T(8,128)(2,1)} async-done(((bf16[1,228,288]{1,2,0:T(8,128)(2,1)}), bf16[32,228,288]{1,2,0:T(8,128)(2,1)}) %all-gather.16.cloned.1.call-update) | async-done | bytes 4202512 | tf_op jit(solution)/shard_map/all_gather | solution.py:402
  194.0 2.0 slice.165
  197.0 3.6 fusion.20
  200.7 4.5 copy.230
  205.1 4.2 copy.231
  209.4 2.7 copy.229
  213.2 61.5 %all-gather.12.cloned.1.call-done = bf16[24,256,384]{2,1,0:T(8,128)(2,1)} async-done(((bf16[3,256,384]{2,1,0:T(8,128)(2,1)}), bf16[24,256,384]{2,1,0:T(8,128)(2,1)}) %all-gather.12.cloned.1.call-update) | async-done | bytes 4718608 | tf_op jit(solution)/shard_map/all_gather | solution.py:526
  274.7 33.3 %shard_map.459 = (bf16[3,256,576]{2,1,0:T(8,128)(2,1)}, f32[3,4,3,192,128]{4,3,2,1,0:T(8,128)}) custom-call(s32[3,32]{1,0:T(4,128)} %reshape.187.blocks_ref, s32[3,4]{1,0:T(4,128)} %copy.225.own_ref, bf16[3,4,3,192,128]{4,3,2,1,0:T(8,128)(2,1)} %get-tuple-element.45.query_ref, bf16[8,3,256,384]{3,2,1,0:T(8,128)(2,1)} %bitcast.180), custom_call_target="tpu_custom_call" | custom-call | flops 3623878656 | bytes 10911744 | tf_op jit(solution)/shard_map/pallas_call | solution.py:373
  308.1 21.3 %shard_map.460 = (f32[3,256,576]{2,1,0:T(8,128)}, bf16[3,256,576]{2,1,0:T(8,128)(2,1)}, bf16[3,256,1536]{2,1,0:T(8,128)(2,1)}, bf16[3,256,1536]{2,1,0:T(8,128)(2...) custom-call(bf16[3,256,576]{2,1,0:T(8,128)(2,1)} %pad_maximum_fusion, ...), custom_call_target="tpu_custom_call" | custom-call | flops 9172942848 | bytes 21906432 | tf_op jit(solution)/shard_map/pallas_call | solution.py:373
  329.4 59.3 %shard_map.461 = (bf16[3,256,576]{2,1,0:T(8,128)(2,1)}, bf16[8,3,256,384]{3,2,1,0:T(8,128)(2,1)}) custom-call(s32[3,32]{1,0:T(4,128)} %reshape.187.blocks_ref, s32[3,4]{1,0:T(4,128)} %copy.225.own_ref, bf16[3,4,3,192,128]{4,3,2,1,0:T(8,128)(2,1)} %get-tuple-element.45.query_ref, bf16[8,3,256,384]{3,2,1,0:T(8,128)(2,1)} %bitcast.181, ...), custom_call_target="tpu_custom_call" | custom-call | flops 9059696640 | bytes 18186240 | tf_op jit(solution)/shard_map/pallas_call | solution.py:373
  390.7 2.8 bitcast_convert_fusion
  393.4 2.6 convert_element_type.68
  396.5 1.5 reshape.206
  398.1 4.5 bitcast_convert_fusion.2
  402.5 2.9 copy.249
  405.4 4.5 bitcast_convert_fusion.1
  409.9 3.9 copy.251
  413.8 2.4 bitcast_convert_fusion.3
  416.5 2.7 pad_maximum_fusion.1
  419.2 1.8 fusion.19
  420.9 3.7 pad_maximum_fusion
  424.7 7.9 reshape.230
  432.6 8.0 copy.253
  444.3 1.7 fusion.23
  446.3 1.2 copy.234
  447.5 34.9 %reduce-scatter.5.cloned.1.call-done = bf16[1,3,256,384]{3,2,1,0:T(8,128)(2,1)} async-done(((bf16[8,3,256,384]{3,2,1,0:T(8,128)(2,1)}), bf16[1,3,256,384]{3,2,1,0:T(8,128)(2,1)}) %reduce-scatter.5.cloned.1.call-update) | async-done | bytes 589840 | tf_op jit(solution)/shard_map/reduce_scatter | solution.py:613
  482.4 6.9 shard_map.462
  489.3 2.5 convolution_bitcast_fusion
  496.4 1.6 reshape.201
  498.2 1.4 constant_dynamic-update-slice_fusion.2
  499.6 1.2 copy-done.6
  501.4 84.2 %reduce-scatter.11.cloned.1.call-done = bf16[1,36,768]{2,1,0:T(8,128)(2,1)} async-done(((bf16[32,36,768]{2,1,0:T(8,128)(2,1)}), bf16[1,36,768]{2,1,0:T(8,128)(2,1)}) %reduce-scatter.11.cloned.1.call-update) | async-done | bytes 55312 | tf_op jit(solution)/shard_map/reduce_scatter | solution.py:412
  585.6 1.8 multiply_subtract_fusion.2
  587.4 109.7 %reduce-scatter.9.cloned.1.call-done = bf16[1,228,288]{1,2,0:T(8,128)(2,1)} async-done(((bf16[32,228,288]{1,2,0:T(8,128)(2,1)}), bf16[1,228,288]{1,2,0:T(8,128)(2,1)}) %reduce-scatter.9.cloned.1.call-update) | async-done | bytes 131344 | tf_op jit(solution)/shard_map/reduce_scatter | solution.py:412
  698.3 2.0 multiply_subtract_fusion
  700.2 1.7 copy.264
  701.9 1.7 copy.265
  706.7 1.5 multiply_subtract_fusion.3
  708.5 1.3 broadcast.141.clone.1
  710.9 2.1 constant_dynamic-update-slice_fusion
  713.1 86.3 %reduce-scatter.7.cloned.1.call-done = bf16[1,62,288]{2,1,0:T(8,128)(2,1)} async-done(((bf16[32,62,288]{2,1,0:T(8,128)(2,1)}), bf16[1,62,288]{2,1,0:T(8,128)(2,1)}) %reduce-scatter.7.cloned.1.call-update) | async-done | bytes 35728 | tf_op jit(solution)/shard_map/reduce_scatter | solution.py:412
  (202 shorter events, 43.9 us)
Async XLA Ops:
  7.2 7.7 copy-start.11
  7.2 7.7 copy-start.10
  7.2 62.1 %all-gather.14.cloned.1.call-start = ((), (), s32[]{:S(2)}) async-start(), calls=%async_computation.9 | async-start | bytes 1622016 | tf_op jit(solution)/shard_map/all_gather | solution.py:402
  10.3 117.6 %all-gather.18.cloned.1.call-start = ((), (), s32[]{:S(2)}) async-start(), calls=%async_computation.11 | async-start | bytes 2027520 | tf_op jit(solution)/shard_map/all_gather | solution.py:402
  11.9 182.0 %all-gather.16.cloned.1.call-start = ((), (), s32[]{:S(2)}) async-start(), calls=%async_computation.10 | async-start | bytes 4866048 | tf_op jit(solution)/shard_map/all_gather | solution.py:402
  14.8 259.9 %all-gather.12.cloned.1.call-start = ((), (), s32[]{:S(2)}) async-start(), calls=%async_computation.8 | async-start | bytes 5308416 | tf_op jit(solution)/shard_map/all_gather | solution.py:526
  14.9 2.1 copy-start.36
  16.2 4.1 collective-permute-start
  73.5 1.0 copy-start.1
  74.6 1.1 slice-start
  75.9 1.5 copy-start.2
  77.4 7.0 copy-start.8
  78.0 8.5 %copy-start.7 = (bf16[3,128,576]{1,2,0:T(8,128)(2,1)S(1)}, bf16[3,128,576]{1,2,0:T(8,128)(2,1)}, u32[]{:S(2)}) copy-start(bf16[3,128,576]{1,2,0:T(8,128)(2,1)} %get-tuple-element.208) | copy-start | bytes 1327108
  84.3 398.1 %reduce-scatter.5.cloned.1.call-start = ((), (), s32[]{:S(2)}) async-start(), calls=%async_computation.4 | async-start | bytes 5308416 | tf_op jit(solution)/shard_map/reduce_scatter | solution.py:613
  84.7 2.1 collective-permute-start.1
  86.7 44.2 %copy-start.4 = (bf16[3,128,576]{2,1,0:T(8,128)(2,1)}, bf16[3,128,576]{2,1,0:T(8,128)(2,1)S(1)}, u32[]{:S(2)}) copy-start(bf16[3,128,576]{2,1,0:T(8,128)(2,1)S(1)} %copy.281) | copy-start | bytes 1327108
  86.7 44.2 %copy-start.15 = (bf16[3,128,576]{2,1,0:T(8,128)(2,1)}, bf16[3,128,576]{2,1,0:T(8,128)(2,1)S(1)}, u32[]{:S(2)}) copy-start(bf16[3,128,576]{2,1,0:T(8,128)(2,1)S(1)} %collective-permute-done.1) | copy-start | bytes 1327108
  194.0 3.0 copy-start
  388.7 1.2 copy-start.16
  388.7 2.0 copy-start.38
  388.7 196.9 %reduce-scatter.11.cloned.1.call-start = ((), (), s32[]{:S(2)}) async-start(), calls=%async_computation.7 | async-start | bytes 2027520 | tf_op jit(solution)/shard_map/reduce_scatter | solution.py:412
  396.5 1.6 copy-start.39
  398.0 299.1 %reduce-scatter.9.cloned.1.call-start = ((), (), s32[]{:S(2)}) async-start(), calls=%async_computation.6 | async-start | bytes 4866048 | tf_op jit(solution)/shard_map/reduce_scatter | solution.py:412
  440.6 1.2 copy-start.19
  440.6 1.3 copy-start.20
  440.6 2.1 copy-start.21
  440.6 2.9 copy-start.22
  440.6 3.6 copy-start.32
  440.7 358.8 %reduce-scatter.7.cloned.1.call-start = ((), (), s32[]{:S(2)}) async-start(), calls=%async_computation.5 | async-start | bytes 1622016 | tf_op jit(solution)/shard_map/reduce_scatter | solution.py:412
  447.5 50.7 %collective-permute-start.2 = (f32[3,128,576]{1,2,0:T(8,128)}, f32[3,128,576]{1,2,0:T(8,128)}, u32[]{:S(2)}, u32[]{:S(2)}) collective-permute-start(f32[3,128,576]{1,2,0:T(8,128)} %copy.234), channel_id=1, source_target_pairs={{0,2},{2,0},{4,6},{6,4},{8,10},{10,8},{12,14},{14,12},{16,18},{18,... | collective-permute-start | bytes 2654216 | tf_op jit(solution)/shard_map/ppermute | solution.py:477
  482.4 6.9 copy-start.37
  498.1 2.7 copy-start.3
  499.6 1.2 copy-start.6
  500.9 197.3 %copy-start.12 = (f32[288,96]{0,1:T(8,128)S(1)}, f32[288,96]{0,1:T(8,128)}, u32[]{:S(2)}) copy-start(f32[288,96]{0,1:T(8,128)} %copy.256) | copy-start | bytes 331780
  501.3 209.6 %collective-permute-start.3 = (f32[3,128,576]{1,2,0:T(8,128)S(1)}, f32[3,128,576]{1,2,0:T(8,128)}, u32[]{:S(2)}, u32[]{:S(2)}) collective-permute-start(f32[3,128,576]{1,2,0:T(8,128)S(1)} %copy.241), channel_id=1, source_target_pairs={{0,2},{2,0},{4,6},{6,4},{8,10},{10,8},{12,14},{14,12},{16,18},{18,... | collective-permute-start | bytes 2654216 | tf_op jit(solution)/shard_map/ppermute | solution.py:477
  698.2 8.4 %copy-start.17 = (f32[288,36]{0,1:T(8,128)S(1)}, f32[288,36]{0,1:T(8,128)}, u32[]{:S(2)}) copy-start(f32[288,36]{0,1:T(8,128)} %param.33) | copy-start | bytes 124420
  709.8 90.4 %copy-start.18 = (f32[288,36]{0,1:T(8,128)S(1)}, f32[288,36]{0,1:T(8,128)}, u32[]{:S(2)}) copy-start(f32[288,36]{0,1:T(8,128)} %param.30) | copy-start | bytes 124420
  709.8 90.4 %copy-start.25 = (f32[288,36]{0,1:T(8,128)S(1)}, f32[288,36]{0,1:T(8,128)}, u32[]{:S(2)}) copy-start(f32[288,36]{0,1:T(8,128)} %param.38) | copy-start | bytes 124420
  709.8 90.4 %copy-start.26 = (f32[288,36]{0,1:T(8,128)S(1)}, f32[288,36]{0,1:T(8,128)}, u32[]{:S(2)}) copy-start(f32[288,36]{0,1:T(8,128)} %param.46) | copy-start | bytes 124420
  709.8 91.1 %copy-start.31 = (f32[288,2]{0,1:T(2,128)S(1)}, f32[288,2]{0,1:T(2,128)}, u32[]{:S(2)}) copy-start(f32[288,2]{0,1:T(2,128)} %param.37) | copy-start | bytes 6916
  709.9 91.1 %copy-start.34 = (f32[288,2]{0,1:T(2,128)S(1)}, f32[288,2]{0,1:T(2,128)}, u32[]{:S(2)}) copy-start(f32[288,2]{0,1:T(2,128)} %param.45) | copy-start | bytes 6916
  709.9 91.1 %copy-start.35 = (f32[288,2]{0,1:T(2,128)S(1)}, f32[288,2]{0,1:T(2,128)}, u32[]{:S(2)}) copy-start(f32[288,2]{0,1:T(2,128)} %param.53) | copy-start | bytes 6916
  709.9 91.7 %copy-start.23 = (f32[288,12]{0,1:T(8,128)S(1)}, f32[288,12]{0,1:T(8,128)}, u32[]{:S(2)}) copy-start(f32[288,12]{0,1:T(8,128)} %param.32) | copy-start | bytes 41476
  709.9 91.7 %copy-start.24 = (f32[288,12]{0,1:T(8,128)S(1)}, f32[288,12]{0,1:T(8,128)}, u32[]{:S(2)}) copy-start(f32[288,12]{0,1:T(8,128)} %param.31) | copy-start | bytes 41476
  709.9 91.7 %copy-start.27 = (f32[288,12]{0,1:T(8,128)S(1)}, f32[288,12]{0,1:T(8,128)}, u32[]{:S(2)}) copy-start(f32[288,12]{0,1:T(8,128)} %param.40) | copy-start | bytes 41476
  709.9 91.7 %copy-start.28 = (f32[288,12]{0,1:T(8,128)S(1)}, f32[288,12]{0,1:T(8,128)}, u32[]{:S(2)}) copy-start(f32[288,12]{0,1:T(8,128)} %param.48) | copy-start | bytes 41476
  709.9 91.7 %copy-start.29 = (f32[288,12]{0,1:T(8,128)S(1)}, f32[288,12]{0,1:T(8,128)}, u32[]{:S(2)}) copy-start(f32[288,12]{0,1:T(8,128)} %param.47) | copy-start | bytes 41476
  709.9 91.6 %copy-start.30 = (f32[288,12]{0,1:T(8,128)S(1)}, f32[288,12]{0,1:T(8,128)}, u32[]{:S(2)}) copy-start(f32[288,12]{0,1:T(8,128)} %param.39) | copy-start | bytes 41476
  (5 other events, 4.7 us)
Sparse Core Ops, SparseCore 0:
  11.5 57.7 all-gather.13
  72.8 55.0 all-gather.17
  131.5 62.4 all-gather.15
  196.0 78.6 all-gather.11
  388.8 93.5 reduce-scatter.4
  487.5 98.0 reduce-scatter.10
  591.1 106.0 reduce-scatter.8
  703.2 96.1 reduce-scatter.6
